TPU v7x, 128 devices: a whole 4x4x4 slice. The times are simulated.
128 devices in a mesh: rows: 8 (over z_lo, x), cols: 16 (over y, z_hi, core).
Axes of the slice: x: 4, y: 4, z: 4 (z_hi: 2, z_lo: 2; z = z_hi * 2 + z_lo), core: 2. Of those that a mesh axis runs over, the one named last changes fastest.
Arguments:
- observed: float32 [32768, 8192], P('rows', 'cols'), may hold values from -8 to 8
- u_start: float32 [32768, 64], P(('rows', 'cols')), may hold values from -3 to 3
- v_start: float32 [8192, 64], P(('cols', 'rows')), may hold values from -3 to 3
Outputs:
- low_rank: float32 [32768, 8192], P('rows', 'cols')
- sparse: float32 [32768, 8192], P('rows', 'cols')
- u_final: float32 [32768, 64], P(('rows', 'cols'))
- v_final: float32 [8192, 64], P(('cols', 'rows'))
All inputs are finite; a program needn't handle non-finite values.
Results may differ from a plain program's by a relative error of at most 0.00014.
Values sent between devices are 32-bit elements; how exact they have to be, the bound alone decides.
A program may use at most 128 MiB of HBM per device.

v0:
```python
import jax
import jax.numpy as jnp
from jax import lax
from jax.sharding import PartitionSpec as P

ITERS = 4


SHRINK = 0.5
RIDGE = 1.0
HI = lax.Precision.HIGHEST


def ridge_solve(part, gram):
    eye = jnp.eye(gram.shape[0], dtype=gram.dtype)
    chol = jnp.linalg.cholesky(gram + RIDGE * eye)
    return jax.scipy.linalg.cho_solve((chol, True), part.T).T


def inner(left, right):
    return lax.dot_general(
        left, right, (((0,), (0,)), ((), ())), precision=HI, preferred_element_type=jnp.float32
    )


def shards(observed, u_start, v_start):
    u_panel = lax.all_gather(u_start, "cols", axis=0, tiled=True)
    v_panel = lax.all_gather(v_start, "rows", axis=0, tiled=True)
    u_own = u_start
    v_own = v_start
    sparse = jnp.zeros_like(observed)
    for step in range(ITERS):
        low = lax.dot_general(
            u_panel,
            v_panel,
            (((1,), (1,)), ((), ())),
            precision=HI,
            preferred_element_type=jnp.float32,
        )
        diff = observed - low
        sparse = diff - jnp.clip(diff, -SHRINK, SHRINK)
        remain = observed - sparse
        gram_v = lax.psum(inner(v_own, v_own), ("rows", "cols"))
        part_u = lax.psum_scatter(
            jnp.dot(remain, v_panel, precision=HI), "cols", scatter_dimension=0, tiled=True
        )
        u_own = ridge_solve(part_u, gram_v)
        u_panel = lax.all_gather(u_own, "cols", axis=0, tiled=True)
        gram_u = lax.psum(inner(u_own, u_own), ("rows", "cols"))
        part_v = lax.psum_scatter(inner(remain, u_panel), "rows", scatter_dimension=0, tiled=True)
        v_own = ridge_solve(part_v, gram_u)
        v_panel = lax.all_gather(v_own, "rows", axis=0, tiled=True)
    low = lax.dot_general(
        u_panel, v_panel, (((1,), (1,)), ((), ())), precision=HI, preferred_element_type=jnp.float32
    )
    return (low, sparse, u_own, v_own)


def solution(mesh):
    return jax.shard_map(
        shards,
        mesh=mesh,
        in_specs=(P("rows", "cols"), P(("rows", "cols"), None), P(("cols", "rows"), None)),
        out_specs=(
            P("rows", "cols"),
            P("rows", "cols"),
            P(("rows", "cols"), None),
            P(("cols", "rows"), None),
        ),
        check_vma=False,
    )
```

profile of v0, /device:TPU:0, one launch (start us, length us, event | category | flops | bytes accessed | tf_op | source)
XLA Modules:
  0.0 1088.2 jit_solution(14704657444312022275)
XLA Ops:
  7.9 29.6 %all_gather.31 = f32[512,64]{1,0:T(8,128)S(1)} all-gather(f32[64,64]{1,0:T(8,128)} %param.10), channel_id=1, replica_groups=mesh['rows'=8,'cols'=16] {'rows'}, dimensions={0}, use_global_device_ids=true | all-gather | bytes 147456 | tf_op jit(solution)/shard_map/all_gather | solution.py:28
  37.5 20.7 %all-gather.6.cloned.1.call-done = f32[4096,64]{0,1:T(8,128)} async-done(((f32[256,64]{0,1:T(8,128)}), f32[4096,64]{0,1:T(8,128)}) %all-gather.6.cloned.1.call-update) | async-done | bytes 1048592 | tf_op jit(solution)/shard_map/all_gather | solution.py:27
  58.2 10.2 fusion
  68.5 3.4 copy-done.3
  71.9 8.1 fusion.72
  80.3 65.8 %psum.56 = f32[64,64]{0,1:T(8,128)S(1)} all-reduce(f32[64,64]{0,1:T(8,128)S(1)} %fusion.71), channel_id=1, replica_groups=mesh['rows'=8,'cols'=16] {'rows','cols'}, use_global_device_ids=true, to_apply=%region_0.1 | all-reduce | flops 4096 | bytes 32768 | tf_op jit(solution)/shard_map/psum | solution.py:43
  146.2 5.8 cholesky.134
  153.4 4.9 custom-call.18
  158.4 1.2 fusion.9
  160.5 1.1 fusion.73
  161.6 64.4 %psum.57 = f32[64,64]{0,1:T(8,128)S(1)} all-reduce(f32[64,64]{0,1:T(8,128)S(1)} %fusion.73), channel_id=1, replica_groups=mesh['rows'=8,'cols'=16] {'rows','cols'}, use_global_device_ids=true, to_apply=%region_4.7 | all-reduce | flops 4096 | bytes 32768 | tf_op jit(solution)/shard_map/psum | solution.py:49
  226.2 5.8 cholesky.145
  232.1 16.4 %fusion.74 = f32[512,64]{1,0:T(8,128)} fusion(f32[4096,512]{1,0:T(8,128)} %copy-done.3, f32[4096,64]{0,1:T(8,128)} %all-gather.8.cloned.1.call-done), kind=kOutput, calls=%fused_computation.116 | convolution fusion | flops 1610612736 | bytes 9568256 | tf_op jit(solution)/shard_map/dot_general | solution.py:21
  250.3 4.9 custom-call.19
  255.2 27.7 %reduce-scatter.11.cloned.1.call-done = f32[64,64]{1,0:T(8,128)} async-done(((f32[512,64]{1,0:T(8,128)}), f32[64,64]{1,0:T(8,128)}) %reduce-scatter.11.cloned.1.call-update) | async-done | bytes 16400 | tf_op jit(solution)/shard_map/reduce_scatter | solution.py:50
  282.8 1.0 fusion.48
  284.1 28.5 %all_gather.33 = f32[512,64]{1,0:T(8,128)S(1)} all-gather(f32[64,64]{1,0:T(8,128)S(1)} %copy.30), channel_id=1, replica_groups=mesh['rows'=8,'cols'=16] {'rows'}, dimensions={0}, use_global_device_ids=true | all-gather | bytes 147456 | tf_op jit(solution)/shard_map/all_gather | solution.py:52
  312.6 10.1 fusion.1
  322.7 3.4 copy-done.1
  326.1 8.1 fusion.76
  334.4 65.0 %psum.58 = f32[64,64]{0,1:T(8,128)S(1)} all-reduce(f32[64,64]{0,1:T(8,128)S(1)} %fusion.75), channel_id=1, replica_groups=mesh['rows'=8,'cols'=16] {'rows','cols'}, use_global_device_ids=true, to_apply=%region_6.10 | all-reduce | flops 4096 | bytes 32768 | tf_op jit(solution)/shard_map/psum | solution.py:43
  399.5 5.8 cholesky.156
  406.7 4.9 custom-call.20
  411.6 1.2 fusion.7
  412.8 0.8 fusion.44
  413.7 1.1 fusion.77
  414.9 63.8 %psum.59 = f32[64,64]{0,1:T(8,128)S(1)} all-reduce(f32[64,64]{0,1:T(8,128)S(1)} %fusion.77), channel_id=1, replica_groups=mesh['rows'=8,'cols'=16] {'rows','cols'}, use_global_device_ids=true, to_apply=%region_8.12 | all-reduce | flops 4096 | bytes 32768 | tf_op jit(solution)/shard_map/psum | solution.py:49
  478.7 5.8 cholesky.167
  484.7 16.4 %fusion.78 = f32[512,64]{1,0:T(8,128)} fusion(f32[4096,512]{1,0:T(8,128)} %copy-done.1, f32[4096,64]{0,1:T(8,128)} %all-gather.10.cloned.1.call-done), kind=kOutput, calls=%fused_computation.120 | convolution fusion | flops 1610612736 | bytes 9568256 | tf_op jit(solution)/shard_map/dot_general | solution.py:21
  502.7 4.9 custom-call.21
  507.6 27.4 %reduce-scatter.15.cloned.1.call-done = f32[64,64]{1,0:T(8,128)} async-done(((f32[512,64]{1,0:T(8,128)}), f32[64,64]{1,0:T(8,128)}) %reduce-scatter.15.cloned.1.call-update) | async-done | bytes 16400 | tf_op jit(solution)/shard_map/reduce_scatter | solution.py:50
  535.0 1.0 fusion.38
  536.3 28.6 %all_gather.35 = f32[512,64]{1,0:T(8,128)S(1)} all-gather(f32[64,64]{1,0:T(8,128)S(1)} %copy.35), channel_id=1, replica_groups=mesh['rows'=8,'cols'=16] {'rows'}, dimensions={0}, use_global_device_ids=true | all-gather | bytes 147456 | tf_op jit(solution)/shard_map/all_gather | solution.py:52
  564.8 10.1 fusion.2
  574.9 3.4 copy-done.2
  578.3 8.1 fusion.80
  586.6 65.0 %psum.60 = f32[64,64]{0,1:T(8,128)S(1)} all-reduce(f32[64,64]{0,1:T(8,128)S(1)} %fusion.79), channel_id=1, replica_groups=mesh['rows'=8,'cols'=16] {'rows','cols'}, use_global_device_ids=true, to_apply=%region_10.14 | all-reduce | flops 4096 | bytes 32768 | tf_op jit(solution)/shard_map/psum | solution.py:43
  651.7 5.8 cholesky.178
  658.9 4.9 custom-call.22
  663.8 1.2 fusion.5
  665.9 1.1 fusion.81
  667.0 63.6 %psum.61 = f32[64,64]{0,1:T(8,128)S(1)} all-reduce(f32[64,64]{0,1:T(8,128)S(1)} %fusion.81), channel_id=1, replica_groups=mesh['rows'=8,'cols'=16] {'rows','cols'}, use_global_device_ids=true, to_apply=%region_12.16 | all-reduce | flops 4096 | bytes 32768 | tf_op jit(solution)/shard_map/psum | solution.py:49
  730.8 5.8 cholesky.189
  736.7 16.4 %fusion.82 = f32[512,64]{1,0:T(8,128)} fusion(f32[4096,512]{1,0:T(8,128)} %copy-done.2, f32[4096,64]{0,1:T(8,128)} %all-gather.12.cloned.1.call-done), kind=kOutput, calls=%fused_computation.124 | convolution fusion | flops 1610612736 | bytes 9568256 | tf_op jit(solution)/shard_map/dot_general | solution.py:21
  754.7 4.9 custom-call.23
  759.6 28.0 %reduce-scatter.19.cloned.1.call-done = f32[64,64]{1,0:T(8,128)} async-done(((f32[512,64]{1,0:T(8,128)}), f32[64,64]{1,0:T(8,128)}) %reduce-scatter.19.cloned.1.call-update) | async-done | bytes 16400 | tf_op jit(solution)/shard_map/reduce_scatter | solution.py:50
  787.6 1.0 fusion.28
  788.8 28.4 %all_gather.37 = f32[512,64]{1,0:T(8,128)S(1)} all-gather(f32[64,64]{1,0:T(8,128)S(1)} %copy.40), channel_id=1, replica_groups=mesh['rows'=8,'cols'=16] {'rows'}, dimensions={0}, use_global_device_ids=true | all-gather | bytes 147456 | tf_op jit(solution)/shard_map/all_gather | solution.py:52
  817.2 12.1 %fusion.70 = (f32[4096,512]{1,0:T(8,128)S(1)}, f32[4096,512]{1,0:T(8,128)}) fusion(f32[4096,512]{1,0:T(8,128)} %param.8, f32[4096,64]{0,1:T(8,128)S(1)} %copy-done.5, f32[512,64]{1,0:T(8,128)S(1)} %all_gather.37), kind=kOutput, calls=%fused_computation.112 | convolution fusion | flops 1619001344 | bytes 26345472 | tf_op jit(solution)/shard_map/dot_general | solution.py:33
  829.3 3.4 copy-done
  832.7 8.1 fusion.84
  841.1 65.2 %psum.62 = f32[64,64]{0,1:T(8,128)S(1)} all-reduce(f32[64,64]{0,1:T(8,128)S(1)} %fusion.83), channel_id=1, replica_groups=mesh['rows'=8,'cols'=16] {'rows','cols'}, use_global_device_ids=true, to_apply=%region_14.18 | all-reduce | flops 4096 | bytes 32768 | tf_op jit(solution)/shard_map/psum | solution.py:43
  906.4 5.8 cholesky.200
  913.6 4.9 custom-call.24
  918.5 1.2 fusion.3
  920.6 1.1 fusion.85
  921.7 63.4 %psum.63 = f32[64,64]{0,1:T(8,128)S(1)} all-reduce(f32[64,64]{0,1:T(8,128)S(1)} %fusion.85), channel_id=1, replica_groups=mesh['rows'=8,'cols'=16] {'rows','cols'}, use_global_device_ids=true, to_apply=%region_16.20 | all-reduce | flops 4096 | bytes 32768 | tf_op jit(solution)/shard_map/psum | solution.py:49
  985.3 5.8 cholesky.211
  991.2 16.4 %fusion.86 = f32[512,64]{1,0:T(8,128)} fusion(f32[4096,512]{1,0:T(8,128)} %copy-done, f32[4096,64]{0,1:T(8,128)} %all-gather.14.cloned.1.call-done), kind=kOutput, calls=%fused_computation.128 | convolution fusion | flops 1610612736 | bytes 9568256 | tf_op jit(solution)/shard_map/dot_general | solution.py:21
  1008.9 4.9 custom-call.25
  1013.8 28.4 %reduce-scatter.23.cloned.1.call-done = f32[64,64]{1,0:T(8,128)} async-done(((f32[512,64]{1,0:T(8,128)}), f32[64,64]{1,0:T(8,128)}) %reduce-scatter.23.cloned.1.call-update) | async-done | bytes 16400 | tf_op jit(solution)/shard_map/reduce_scatter | solution.py:50
  1042.2 1.0 fusion.19
  1043.5 28.8 %all_gather.39 = f32[512,64]{1,0:T(8,128)S(1)} all-gather(f32[64,64]{1,0:T(8,128)S(1)} %copy.43), channel_id=1, replica_groups=mesh['rows'=8,'cols'=16] {'rows'}, dimensions={0}, use_global_device_ids=true | all-gather | bytes 147456 | tf_op jit(solution)/shard_map/all_gather | solution.py:52
  1072.3 9.0 fusion.87
  (113 shorter events, 18.0 us)
Async XLA Ops:
  7.2 51.1 %all-gather.6.cloned.1.call-start = ((), (), s32[]{:S(2)}) async-start(), calls=%async_computation.8 | async-start | bytes 1114112 | tf_op jit(solution)/shard_map/all_gather | solution.py:27
  7.9 150.5 %reduce-scatter.9.cloned.1.call-start = ((), (), s32[]{:S(2)}) async-start(), calls=%async_computation.9 | async-start | bytes 2228224 | tf_op jit(solution)/shard_map/reduce_scatter | solution.py:44
  68.5 3.4 copy-start.3
  71.9 8.2 copy-start.8
  80.0 152.1 %all-gather.8.cloned.1.call-start = ((), (), s32[]{:S(2)}) async-start(), calls=%async_computation.10 | async-start | bytes 1114112 | tf_op jit(solution)/shard_map/all_gather | solution.py:48
  160.4 122.4 %reduce-scatter.11.cloned.1.call-start = ((), (), s32[]{:S(2)}) async-start(), calls=%async_computation.11 | async-start | bytes 294912 | tf_op jit(solution)/shard_map/reduce_scatter | solution.py:50
  232.1 80.6 %copy-start.6 = (f32[4096,64]{0,1:T(8,128)S(1)}, f32[4096,64]{0,1:T(8,128)}, u32[]{:S(2)}) copy-start(f32[4096,64]{0,1:T(8,128)} %all-gather.8.cloned.1.call-done) | copy-start | bytes 3145732
  248.5 163.1 %reduce-scatter.13.cloned.1.call-start = ((), (), s32[]{:S(2)}) async-start(), calls=%async_computation.12 | async-start | bytes 2228224 | tf_op jit(solution)/shard_map/reduce_scatter | solution.py:44
  322.7 3.4 copy-start.1
  334.2 150.4 %all-gather.10.cloned.1.call-start = ((), (), s32[]{:S(2)}) async-start(), calls=%async_computation.13 | async-start | bytes 1114112 | tf_op jit(solution)/shard_map/all_gather | solution.py:48
  413.7 121.3 %reduce-scatter.15.cloned.1.call-start = ((), (), s32[]{:S(2)}) async-start(), calls=%async_computation.14 | async-start | bytes 294912 | tf_op jit(solution)/shard_map/reduce_scatter | solution.py:50
  484.6 80.2 %copy-start.7 = (f32[4096,64]{0,1:T(8,128)S(1)}, f32[4096,64]{0,1:T(8,128)}, u32[]{:S(2)}) copy-start(f32[4096,64]{0,1:T(8,128)} %all-gather.10.cloned.1.call-done) | copy-start | bytes 3145732
  501.1 162.7 %reduce-scatter.17.cloned.1.call-start = ((), (), s32[]{:S(2)}) async-start(), calls=%async_computation.15 | async-start | bytes 2228224 | tf_op jit(solution)/shard_map/reduce_scatter | solution.py:44
  574.9 3.4 copy-start.2
  586.4 150.3 %all-gather.12.cloned.1.call-start = ((), (), s32[]{:S(2)}) async-start(), calls=%async_computation.16 | async-start | bytes 1114112 | tf_op jit(solution)/shard_map/all_gather | solution.py:48
  665.9 121.7 %reduce-scatter.19.cloned.1.call-start = ((), (), s32[]{:S(2)}) async-start(), calls=%async_computation.17 | async-start | bytes 294912 | tf_op jit(solution)/shard_map/reduce_scatter | solution.py:50
  736.7 80.5 %copy-start.5 = (f32[4096,64]{0,1:T(8,128)S(1)}, f32[4096,64]{0,1:T(8,128)}, u32[]{:S(2)}) copy-start(f32[4096,64]{0,1:T(8,128)} %all-gather.12.cloned.1.call-done) | copy-start | bytes 3145732
  753.2 165.3 %reduce-scatter.21.cloned.1.call-start = ((), (), s32[]{:S(2)}) async-start(), calls=%async_computation.18 | async-start | bytes 2228224 | tf_op jit(solution)/shard_map/reduce_scatter | solution.py:44
  829.3 3.4 copy-start
  840.9 150.3 %all-gather.14.cloned.1.call-start = ((), (), s32[]{:S(2)}) async-start(), calls=%async_computation.19 | async-start | bytes 1114112 | tf_op jit(solution)/shard_map/all_gather | solution.py:48
  920.5 121.7 %reduce-scatter.23.cloned.1.call-start = ((), (), s32[]{:S(2)}) async-start(), calls=%async_computation.20 | async-start | bytes 294912 | tf_op jit(solution)/shard_map/reduce_scatter | solution.py:50
  991.2 81.1 %copy-start.4 = (f32[4096,64]{0,1:T(8,128)S(1)}, f32[4096,64]{0,1:T(8,128)}, u32[]{:S(2)}) copy-start(f32[4096,64]{0,1:T(8,128)} %all-gather.14.cloned.1.call-done) | copy-start | bytes 3145732
  1043.5 37.8 %copy-start.9 = (f32[64,64]{1,0:T(8,128)}, f32[64,64]{1,0:T(8,128)S(1)}, u32[]{:S(2)}) copy-start(f32[64,64]{1,0:T(8,128)S(1)} %copy.43) | copy-start | bytes 49156
Sparse Core Ops, SparseCore 0:
  10.3 47.9 all-gather.5
  80.1 69.6 reduce-scatter.8
  160.5 42.9 all-gather.7
  248.6 34.1 reduce-scatter.10
  334.3 69.8 reduce-scatter.12
  413.8 42.2 all-gather.9
  501.2 33.7 reduce-scatter.14
  586.5 69.7 reduce-scatter.16
  666.0 42.5 all-gather.11
  753.3 34.2 reduce-scatter.18
  841.0 69.8 reduce-scatter.20
  920.7 41.9 all-gather.13
  1007.8 34.4 reduce-scatter.22
where the time goes:
time: 1100 us; the launch traced here: 1090 us
  blocking collectives  660 us (60%)
  matrix products  167 us (15%)
  waiting for transfers between devices  133 us (12%)
  other arithmetic  96.7 us (9%)
  between operations  14.9 us (1%)
  local copies, waits for them, and re-layouts  14.5 us (1%)
    psum x4, blocking collectives, shards(): gram_v = lax.psum(inner(v_own, v_own), ('rows', 'cols'))  261 us
    psum x4, blocking collectives, shards(): gram_u = lax.psum(inner(u_own, u_own), ('rows', 'cols'))  255 us
    all_gather x4, blocking collectives, shards(): v_panel = lax.all_gather(v_own, 'rows', axis=0, tiled=True)  114 us
    reduce_scatter x4, waiting for transfers between devices, shards(): lax.psum_scatter(inner(remain, u_panel), 'rows', scatter_dimension=0, til...  111 us
    dot_general x12, matrix products, inner(): lax.dot_general(left, right, (((0,), (0,)), ((), ())), precision=HI, pref...  71 us
    another operation x24, other arithmetic, ridge_solve(): chol = jnp.linalg.cholesky(gram + RIDGE * eye)  52.1 us
    dot_general x5, matrix products, shards(): lax.dot_general(u_panel, v_panel, (((1,), (1,)), ((), ())), precision=HI,...  51.5 us
    another operation x16, other arithmetic, ridge_solve(): return jax.scipy.linalg.cho_solve((chol, True), part.T).T  44.4 us
  transfers between devices with their start and end apart: 13, of which 5 were waited for; matrix products, arithmetic and copies ran while one was open for 9% of the time, Pallas kernels for 0%

commit v1 on v0

v1 whole, which is shorter than its diff:
```python
import functools

import jax
import jax.numpy as jnp
from jax import lax
from jax.experimental import pallas as pl
from jax.experimental.pallas import tpu as pltpu
from jax.sharding import PartitionSpec as P

ITERS = 4
SHRINK = 0.5
RIDGE = 1.0
RANK = 64
NY = 4
NR = 8
CH = 256
HALF = CH // 2
NT_LOC = 512
NS_LOC = 4096
MESH = pl.DeviceIdType.MESH
HI = lax.Precision.HIGHEST
F32 = jnp.float32
BF16 = jnp.bfloat16


def dot(a, b, dims=((1,), (0,)), precision=None):
    return lax.dot_general(a, b, (dims, ((), ())), precision=precision, preferred_element_type=F32)


def lanes(shape):
    return lax.broadcasted_iota(jnp.int32, shape, len(shape) - 1)


def sublanes(shape):
    return lax.broadcasted_iota(jnp.int32, shape, len(shape) - 2)


def roll64(m):
    return pltpu.roll(m, 64, 1)


def pack_gram(m):
    s = m + roll64(m)
    t = s[:64] + s[64:]
    return jnp.where(lanes((32, 128)) < 64, t[:32], t[32:])


def unpack_gram(k):
    kr = roll64(k)
    left = lanes((32, 128)) < 64
    return jnp.concatenate([jnp.where(left, k, kr), jnp.where(left, kr, k)], axis=0)


def twin_eye():
    return jnp.where((lanes((64, 128)) % 64) == sublanes((64, 128)), 1.0, 0.0).astype(F32)


def ridge_inverse(gg):
    eye = twin_eye()
    left = lanes((64, 128)) < 64
    rows = sublanes((64, 128))
    m = jnp.where(left, gg + RIDGE * eye, eye)
    for k in range(RANK):
        col = jnp.broadcast_to(m[:, k : k + 1], (64, 128))
        prow = m[k : k + 1, :] / col[k : k + 1, :]
        m = jnp.where(rows == k, prow, m - col * prow)
    return jnp.where(left, roll64(m), m)


def apply_weights(inv2):
    zero = jnp.zeros_like(inv2)
    return jnp.concatenate(
        [jnp.concatenate([inv2, zero], axis=1), jnp.concatenate([zero, inv2], axis=1)], axis=0
    )


def split(x):
    hi = x.astype(BF16)
    return hi, (x - hi.astype(F32)).astype(BF16)


def factor_kernel(
    obs_hbm, u0_ref, v0_ref,
    ust, vst, u_out, v_out,
    obs, rh, rl, part, r1, r2, a2, r3, pan, gb, qt2, gu, wl, wr, qs, rq, rg, qp, vn,
    gv1, gv2, gv3, gva,
    obs_sem, s1s, s1r, s2s, s2r, s3s, s3r, azs, azr, ays, ayr, acs, acr,
    g1s, g1r, g2s, g2r, g3s, g3r, qs_s, qs_r, rg_s, rg_r, qa_s, qa_r, v0s, v0r,
):
    row = lax.axis_index("rows")
    col = lax.axis_index("cols")
    y, zh, co = col // 4, (col // 2) % 2, col % 2

    def cid(yy, zz, cc):
        return yy * 4 + zz * 2 + cc

    def pos(cc, yy, zz):
        return cc * 8 + yy * 2 + zz

    sib = {"cols": cid(y, zh, 1 - co)}
    zpeer = {"cols": cid(y, 1 - zh, co)}

    def ypeer(d):
        return {"cols": cid(lax.rem(y + d, NY), zh, co)}

    def rpeer(d):
        return {"rows": lax.rem(row + d, NR)}

    def rcopy(src, dst, ssem, rsem, dev):
        return pltpu.make_async_remote_copy(
            src_ref=src, dst_ref=dst, send_sem=ssem, recv_sem=rsem, device_id=dev, device_id_type=MESH
        )

    load = pltpu.make_async_copy(obs_hbm, obs, obs_sem)
    load.start()

    barrier = pltpu.get_barrier_semaphore()
    peers = [sib, zpeer] + [ypeer(d) for d in range(1, NY)] + [rpeer(d) for d in range(1, NR)]
    for dev in peers:
        pl.semaphore_signal(barrier, inc=1, device_id=dev, device_id_type=MESH)
    pl.semaphore_wait(barrier, len(peers))

    own = pos(co, y, zh)
    left128 = lanes((HALF, 128)) < 64
    left256 = (lanes((HALF, 256)) % 128) < 64

    def apply_chunk(slot, j, buf):
        u2 = dot(pan[slot], gb[...], precision=HI)
        hi, lo = split(u2)
        st = jnp.where(left256, hi.astype(F32), lo.astype(F32)).astype(BF16)
        base = pl.multiple_of(j * CH, CH)
        ust[buf, pl.ds(base, HALF), :] = st[:, :128]
        ust[buf, pl.ds(base + HALF, HALF), :] = st[:, 128:]

    def time_chunk(slot, j, buf):
        apply_chunk(slot, j, buf)
        rows = pl.ds(pl.multiple_of(j * CH, CH), CH)
        us = ust[buf, rows, :]
        ut = us.T
        gu[...] += dot(ut, us)
        qt2[...] += dot(ut, rh[rows, :]) + dot(ut, rl[rows, :])

    def gather_cols(process, buf):
        rcopy(pan.at[own], pan.at[own], azs, azr, zpeer).start()
        for d in range(1, NY):
            rcopy(pan.at[own], pan.at[own], ays.at[d - 1, 0], ayr.at[d - 1, 0], ypeer(d)).start()
        rcopy(pan.at[own], pan.at[own], acs.at[y * 2 + zh], acr.at[y * 2 + zh], sib).start()
        process(own, cid(y, zh, co), buf)
        pz = pos(co, y, 1 - zh)
        rcopy(pan.at[pz], pan.at[pz], azs, azr, zpeer).wait_recv()
        for d in range(1, NY):
            rcopy(pan.at[pz], pan.at[pz], ays.at[d - 1, 1], ayr.at[d - 1, 1], ypeer(d)).start()
        rcopy(pan.at[pz], pan.at[pz], acs.at[y * 2 + 1 - zh], acr.at[y * 2 + 1 - zh], sib).start()
        process(pz, cid(y, 1 - zh, co), buf)

        def from_y(i, carry):
            yy = lax.rem(y + 2 * NY - 1 - i, NY)
            for e in range(2):
                zz = zh if e == 0 else 1 - zh
                p = pos(co, yy, zz)
                rcopy(pan.at[p], pan.at[p], ays.at[i, e], ayr.at[i, e], zpeer).wait_recv()
                rcopy(pan.at[p], pan.at[p], acs.at[yy * 2 + zz], acr.at[yy * 2 + zz], sib).start()
                process(p, cid(yy, zz, co), buf)
            return carry

        lax.fori_loop(0, NY - 1, from_y, 0)

        def from_sib(i, carry):
            yy = lax.rem(y + 2 * NY - i // 2, NY)
            zz = lax.rem(zh + i, 2)
            p = pos(1 - co, yy, zz)
            rcopy(pan.at[p], pan.at[p], acs.at[yy * 2 + zz], acr.at[yy * 2 + zz], sib).wait_recv()
            process(p, cid(yy, zz, 1 - co), buf)
            return carry

        lax.fori_loop(0, 2 * NY, from_sib, 0)
        rcopy(pan.at[own], pan.at[own], azs, azr, zpeer).wait_send()

        def drain_y(i, carry):
            for e in range(2):
                rcopy(pan.at[own], pan.at[own], ays.at[i, e], ayr.at[i, e], zpeer).wait_send()
            return carry

        lax.fori_loop(0, NY - 1, drain_y, 0)

        def drain_sib(i, carry):
            rcopy(pan.at[own], pan.at[own], acs.at[i], acr.at[i], sib).wait_send()
            return carry

        lax.fori_loop(0, 2 * NY, drain_sib, 0)

    def set_time(vt, buf):
        vh, vl = split(vt)
        vst[buf, :, :] = jnp.concatenate([vh, vh, vl, vl], axis=0)
        x = jnp.concatenate([vh.astype(F32), vl.astype(F32)], axis=0).T
        xr = roll64(x)
        left = lanes((NT_LOC, 128)) < 64
        zero = jnp.zeros_like(x)
        wl[...] = jnp.concatenate([jnp.where(left, x, zero), jnp.where(left, xr, zero)], axis=1).astype(BF16)
        wr[...] = jnp.concatenate([jnp.where(left, zero, xr), jnp.where(left, zero, x)], axis=1).astype(BF16)
        pair = jnp.concatenate([vh, vl], axis=0)
        gva[...] = pack_gram(dot(pair, pair, dims=((1,), (1,))))

    def series_chunk(slot, j, buf):
        rows = pl.ds(pl.multiple_of(j * CH, CH), CH)
        us = ust[buf, rows, :]
        low = dot(jnp.concatenate([us, us], axis=1), vst[buf, :, :])
        remain = low + jnp.clip(obs[rows, :] - low, -SHRINK, SHRINK)
        hi, lo = split(remain)
        rh[rows, :] = hi
        rl[rows, :] = lo
        a = dot(jnp.concatenate([hi[:HALF], lo[:HALF]], axis=0), wl[...])
        b = dot(jnp.concatenate([hi[HALF:], lo[HALF:]], axis=0), wr[...])
        s = a + b
        s = s[:, :128] + s[:, 128:]
        part[slot] = s[:HALF] + s[HALF:]

    vn[row] = v0_ref[...]
    for d in range(1, NR):
        rcopy(v0_ref, vn.at[row], v0s.at[d - 1], v0r.at[d - 1], rpeer(d)).start()
    pan[own] = u0_ref[...]
    gb[...] = apply_weights(twin_eye())
    gather_cols(apply_chunk, 0)
    for d in range(1, NR):
        src = lax.rem(row + NR - d, NR)
        rcopy(v0_ref, vn.at[src], v0s.at[d - 1], v0r.at[d - 1], rpeer(d)).wait()
    vt0 = vn[...].reshape(NT_LOC, 128).T
    set_time(vt0[:64], 0)
    load.wait()

    def iteration(t, carry):
        buf = lax.rem(t, 2)
        nxt = 1 - buf
        rcopy(gva, gv1, g1s, g1r, sib).start()

        def to_sib(i, c):
            yy = lax.rem(y + 1 + i, NY)
            for zz in range(2):
                series_chunk(pos(1 - co, yy, zz), cid(yy, zz, 1 - co), buf)
            block = pl.ds(pos(1 - co, yy, 0), 2)
            rcopy(part.at[block], r1.at[pl.ds(yy * 2, 2)], s1s.at[i], s1r.at[i], sib).start()
            return c

        lax.fori_loop(0, NY, to_sib, 0)
        rcopy(gva, gv1, g1s, g1r, sib).wait()
        gva[...] += gv1[...]
        for d in range(1, NY):
            rcopy(gva, gv2.at[d - 1], g2s.at[d - 1], g2r.at[d - 1], ypeer(d)).start()

        def own_core(i):
            yy = lax.rem(y + 1 + i, NY)
            for zz in range(2):
                series_chunk(pos(co, yy, zz), cid(yy, zz, co), buf)
            block = pl.ds(pos(co, yy, 0), 2)
            other = r1.at[pl.ds(yy * 2, 2)]
            rcopy(part.at[block], other, s1s.at[i], s1r.at[i], sib).wait_recv()
            part[block] += other[...]
            return yy, block

        def to_y(i, c):
            yy, block = own_core(i)
            rcopy(part.at[block], r2.at[i], s2s.at[i], s2r.at[i], {"cols": cid(yy, zh, co)}).start()
            return c

        lax.fori_loop(0, NY - 1, to_y, 0)
        _, mine = own_core(NY - 1)

        for d in range(1, NY):
            rcopy(gva, gv2.at[d - 1], g2s.at[d - 1], g2r.at[d - 1], ypeer(d)).wait()
        gva[...] += gv2[0] + gv2[1] + gv2[2]
        rcopy(gva, gv3, g3s, g3r, zpeer).start()

        for i in range(NY - 1):
            rcopy(part.at[mine], r2.at[i], s2s.at[i], s2r.at[i], zpeer).wait_recv()
        a2[...] = part[mine] + r2[0] + r2[1] + r2[2]
        hop = rcopy(a2.at[1 - zh], r3, s3s, s3r, zpeer)
        hop.start()
        rcopy(gva, gv3, g3s, g3r, zpeer).wait()
        inv_v = ridge_inverse(unpack_gram(gva[...] + gv3[...]))
        gb[...] = apply_weights(inv_v)
        hop.wait()
        pan[own] = a2[zh] + r3[...]

        def drain(i, c):
            rcopy(part.at[mine], r1.at[pl.ds(0, 2)], s1s.at[i], s1r.at[i], sib).wait_send()
            return c

        lax.fori_loop(0, NY, drain, 0)
        for i in range(NY - 1):
            rcopy(part.at[mine], r2.at[i], s2s.at[i], s2r.at[i], zpeer).wait_send()

        gu[...] = jnp.zeros_like(gu)
        qt2[...] = jnp.zeros_like(qt2)
        gather_cols(time_chunk, nxt)

        q = qt2[...]
        qs[...] = (q[:64] + q[64:]).reshape(NR, 8, NT_LOC)
        gva[...] = pack_gram(gu[...])
        for d in range(1, NR):
            peer = lax.rem(row + d, NR)
            rcopy(qs.at[peer], rq.at[d - 1], qs_s.at[d - 1], qs_r.at[d - 1], rpeer(d)).start()
            rcopy(gva, rg.at[d - 1], rg_s.at[d - 1], rg_r.at[d - 1], rpeer(d)).start()
        acc = qs[row]
        g = gva[...]
        for d in range(1, NR):
            peer = lax.rem(row + d, NR)
            rcopy(qs.at[peer], rq.at[d - 1], qs_s.at[d - 1], qs_r.at[d - 1], rpeer(d)).wait()
            acc += rq[d - 1]
        for d in range(1, NR):
            rcopy(gva, rg.at[d - 1], rg_s.at[d - 1], rg_r.at[d - 1], rpeer(d)).wait()
            g += rg[d - 1]
        qp[row] = acc
        for d in range(1, NR):
            rcopy(qp.at[row], qp.at[row], qa_s.at[d - 1], qa_r.at[d - 1], rpeer(d)).start()
        inv_u = ridge_inverse(unpack_gram(g))
        for d in range(1, NR):
            src = lax.rem(row + NR - d, NR)
            rcopy(qp.at[row], qp.at[src], qa_s.at[d - 1], qa_r.at[d - 1], rpeer(d)).wait()
        vt = dot(inv_u[:, :64], qp[...].reshape(RANK, NT_LOC), precision=HI)
        vn[...] = jnp.concatenate([vt, vt], axis=0).T.reshape(NR, 64, 128)
        set_time(vt, nxt)
        return carry

    lax.fori_loop(0, ITERS, iteration, 0)

    u2 = dot(pan[own], gb[...], precision=HI)
    u_out[pl.ds(0, HALF), :] = u2[:, :RANK]
    u_out[pl.ds(HALF, HALF), :] = u2[:, 128 : 128 + RANK]
    v_out[...] = vn[row][:, :RANK]


def factors(observed, u2, v2):
    vm = pl.BlockSpec(memory_space=pltpu.VMEM)
    dma = pltpu.SemaphoreType.DMA
    return pl.pallas_call(
        factor_kernel,
        out_shape=(
            jax.ShapeDtypeStruct((2, NS_LOC, 128), BF16),
            jax.ShapeDtypeStruct((2, 256, NT_LOC), BF16),
            jax.ShapeDtypeStruct((CH, RANK), F32),
            jax.ShapeDtypeStruct((64, RANK), F32),
        ),
        in_specs=[pl.BlockSpec(memory_space=pl.ANY), vm, vm],
        out_specs=(vm, vm, vm, vm),
        scratch_shapes=[
            pltpu.VMEM((NS_LOC, NT_LOC), F32),
            pltpu.VMEM((NS_LOC, NT_LOC), BF16),
            pltpu.VMEM((NS_LOC, NT_LOC), BF16),
            pltpu.VMEM((16, HALF, 128), F32),
            pltpu.VMEM((8, HALF, 128), F32),
            pltpu.VMEM((3, 2, HALF, 128), F32),
            pltpu.VMEM((2, HALF, 128), F32),
            pltpu.VMEM((HALF, 128), F32),
            pltpu.VMEM((16, HALF, 128), F32),
            pltpu.VMEM((128, 256), F32),
            pltpu.VMEM((128, NT_LOC), F32),
            pltpu.VMEM((128, 128), F32),
            pltpu.VMEM((NT_LOC, 256), BF16),
            pltpu.VMEM((NT_LOC, 256), BF16),
            pltpu.VMEM((NR, 8, NT_LOC), F32),
            pltpu.VMEM((NR - 1, 8, NT_LOC), F32),
            pltpu.VMEM((NR - 1, 32, 128), F32),
            pltpu.VMEM((NR, 8, NT_LOC), F32),
            pltpu.VMEM((NR, 64, 128), F32),
            pltpu.VMEM((32, 128), F32),
            pltpu.VMEM((3, 32, 128), F32),
            pltpu.VMEM((32, 128), F32),
            pltpu.VMEM((32, 128), F32),
            dma,
            dma((4,)), dma((4,)), dma((3,)), dma((3,)), dma, dma,
            dma, dma, dma((3, 2)), dma((3, 2)), dma((8,)), dma((8,)),
            dma, dma, dma((3,)), dma((3,)), dma, dma,
            dma((7,)), dma((7,)), dma((7,)), dma((7,)), dma((7,)), dma((7,)), dma((7,)), dma((7,)),
        ],
        compiler_params=pltpu.CompilerParams(
            collective_id=0, has_side_effects=True, vmem_limit_bytes=52 * 1024 * 1024
        ),
        name="factor_updates",
    )(observed, u2, v2)


def slabs_kernel(obs_ref, u_ref, v_ref, low_ref, sparse_ref):
    def low(k):
        us = u_ref[k]
        return dot(jnp.concatenate([us, us], axis=1), v_ref[k])

    low_ref[...] = low(0)
    diff = obs_ref[...] - low(1)
    sparse_ref[...] = diff - jnp.clip(diff, -SHRINK, SHRINK)


def slabs(observed, ust, vst):
    block = 512
    wide = pl.BlockSpec((block, NT_LOC), lambda i: (i, 0))
    return pl.pallas_call(
        slabs_kernel,
        grid=(NS_LOC // block,),
        out_shape=(jax.ShapeDtypeStruct((NS_LOC, NT_LOC), F32),) * 2,
        in_specs=[
            wide,
            pl.BlockSpec((2, block, 128), lambda i: (0, i, 0)),
            pl.BlockSpec((2, 256, NT_LOC), lambda i: (0, 0, 0)),
        ],
        out_specs=(wide, wide),
        compiler_params=pltpu.CompilerParams(vmem_limit_bytes=40 * 1024 * 1024),
        name="final_slabs",
    )(observed, ust, vst)


def shards(observed, u_start, v_start):
    u2 = jnp.concatenate([u_start[:HALF], u_start[HALF:]], axis=1)
    v2 = jnp.concatenate([v_start, v_start], axis=1)
    ust, vst, u_own, v_own = factors(observed, u2, v2)
    low, sparse = slabs(observed, ust, vst)
    return (low, sparse, u_own, v_own)


def solution(mesh):
    return jax.shard_map(
        shards,
        mesh=mesh,
        in_specs=(P("rows", "cols"), P(("rows", "cols"), None), P(("cols", "rows"), None)),
        out_specs=(
            P("rows", "cols"),
            P("rows", "cols"),
            P(("rows", "cols"), None),
            P(("cols", "rows"), None),
        ),
        check_vma=False,
    )
```

time: 1100 us -> 236 us (0.21)
  blocking collectives: 660 us -> 0 us
  Pallas kernels: 0 us -> 226 us
  matrix products: 167 us -> 0 us
  waiting for transfers between devices: 133 us -> 0 us
  other arithmetic: 96.7 us -> 1 us
  between operations: 14.9 us -> 0.66 us
    psum x8 -> x0, blocking collectives: 516 us -> none  [the longest x4 261 us: shards(): gram_v = lax.psum(inner(v_own, v_own), ('rows', 'cols'))]
    pallas_call x0 -> x2, Pallas kernels: none -> 226 us  [the longest x1 219 us: factors(): pl.pallas_call(factor_kernel, out_shape=(jax.ShapeDtypeStruct((2, NS_LOC,...]
    dot_general x21 -> x0, matrix products: 155 us -> none  [the longest x12 71 us: inner(): lax.dot_general(left, right, (((0,), (0,)), ((), ())), precision=HI, pref...]
    all_gather x5 -> x0, blocking collectives: 144 us -> none  [the longest x4 114 us: shards(): v_panel = lax.all_gather(v_own, 'rows', axis=0, tiled=True)]
    reduce_scatter x8 -> x0, waiting for transfers between devices: 112 us -> none  [the longest x4 111 us: shards(): lax.psum_scatter(inner(remain, u_panel), 'rows', scatter_dimension=0, til...]
    another operation x40 -> x0, other arithmetic: 96.5 us -> none  [the longest x24 52.1 us: ridge_solve(): chol = jnp.linalg.cholesky(gram + RIDGE * eye)]
    all_gather x5 -> x0, waiting for transfers between devices: 20.8 us -> none  [the longest x1 20.7 us: shards(): u_panel = lax.all_gather(u_start, 'cols', axis=0, tiled=True)]
    another operation x16 -> x0, matrix products: 12.7 us -> none  [ridge_solve(): return jax.scipy.linalg.cho_solve((chol, True), part.T).T]
  transfers between devices with their start and end apart: 13 -> 0, of which waited for: 5 -> 0; matrix products, arithmetic and copies ran while one was open for 9% -> 0% of each run, Pallas kernels for 0% -> 0%
where the time goes in v1:
time: 236 us; the launch traced here: 235 us
  Pallas kernels  226 us (96%)
  local copies, waits for them, and re-layouts  7.27 us (3%)
    pallas_call x1, Pallas kernels, factors(): pl.pallas_call(factor_kernel, out_shape=(jax.ShapeDtypeStruct((2, NS_LOC,...  219 us
    pallas_call x1, Pallas kernels, slabs(): pl.pallas_call(slabs_kernel, grid=(NS_LOC // block,), out_shape=(jax.Shap...  7.2 us
    unnamed x8, local copies, waits for them, and re-layouts  6.48 us

profile of v1, /device:TPU:0, one launch (start us, length us, event | category | flops | bytes accessed | tf_op | source)
XLA Modules:
  0.0 235.2 jit_solution(14819829073061113248)
XLA Ops:
  0.6 0.9 pad_maximum_fusion.1.v0_ref
  1.5 0.8 fusion
  2.3 0.1 copy.10
  2.4 0.1 copy.11
  2.5 0.1 pad_maximum_fusion.u0_ref
  2.6 219.1 %factor_updates.1 = (bf16[2,4096,128]{2,1,0:T(8,128)(2,1)}, bf16[2,256,512]{2,1,0:T(8,128)(2,1)S(1)}, f32[256,64]{1,0:T(8,128)S(1)}, f32[64,64]{1,0:T(8,128)S(1)}) custom-call(f32[4096,512]{1,0:T(8,128)} %obs_ref.1, f32[128,128]{1,0:T(8,128)S(1)} %pad_maximum_fusion.u0_ref, f32[64,128]{1,0:T(8,128)S(1)} %pad_maximum_fusion.1.v0_ref), custom_call_target="tpu_custom_call" | custom-call | tf_op jit(solution)/shard_map/factor_updates/pallas_call | solution.py:335
  221.7 0.7 copy.9
  222.4 0.0 copy-start
  222.4 3.4 %copy-done = f32[4096,512]{1,0:T(8,128)S(1)} copy-done((f32[4096,512]{1,0:T(8,128)S(1)}, f32[4096,512]{1,0:T(8,128)}, u32[]{:S(2)}) %copy-start) | copy-done | bytes 8388632
  225.8 0.0 copy-start.1
  225.8 1.6 copy-done.1
  227.4 7.2 %final_slabs.1 = (f32[4096,512]{1,0:T(8,128)}, f32[4096,512]{1,0:T(8,128)}) custom-call(f32[4096,512]{1,0:T(8,128)S(1)} %copy-done, bf16[2,4096,128]{2,1,0:T(8,128)(2,1)S(1)} %copy-done.1, bf16[2,256,512]{2,1,0:T(8,128)(2,1)S(1)} %get-tuple-element.11.v_ref), custom_call_target="tpu_custom_call" | custom-call | tf_op jit(solution)/shard_map/final_slabs/pallas_call | solution.py:395
  234.6 0.6 copy.13
Async XLA Ops:
  222.4 3.4 %copy-start = (f32[4096,512]{1,0:T(8,128)S(1)}, f32[4096,512]{1,0:T(8,128)}, u32[]{:S(2)}) copy-start(f32[4096,512]{1,0:T(8,128)} %obs_ref.1) | copy-start | bytes 25165828
  225.8 1.6 copy-start.1

commit v2 on v1

v2 whole, which is shorter than its diff:
```python
import functools

import jax
import jax.numpy as jnp
from jax import lax
from jax.experimental import pallas as pl
from jax.experimental.pallas import tpu as pltpu
from jax.sharding import PartitionSpec as P

ITERS = 4
SHRINK = 0.5
RIDGE = 1.0
RANK = 64
NY = 4
NR = 8
CH = 256
HALF = CH // 2
NT_LOC = 512
NS_LOC = 4096
FACTOR_VMEM = 34
SLABS_VMEM = 24
MESH = pl.DeviceIdType.MESH
HI = lax.Precision.HIGHEST
F32 = jnp.float32
BF16 = jnp.bfloat16


def dot(a, b, dims=((1,), (0,)), precision=None):
    return lax.dot_general(a, b, (dims, ((), ())), precision=precision, preferred_element_type=F32)


def lanes(shape):
    return lax.broadcasted_iota(jnp.int32, shape, len(shape) - 1)


def sublanes(shape):
    return lax.broadcasted_iota(jnp.int32, shape, len(shape) - 2)


def roll64(m):
    return pltpu.roll(m, 64, 1)


def pack_gram(m):
    s = m + roll64(m)
    t = s[:64] + s[64:]
    return jnp.where(lanes((32, 128)) < 64, t[:32], t[32:])


def unpack_gram(k):
    kr = roll64(k)
    left = lanes((32, 128)) < 64
    return jnp.concatenate([jnp.where(left, k, kr), jnp.where(left, kr, k)], axis=0)


def twin_eye():
    return jnp.where((lanes((64, 128)) % 64) == sublanes((64, 128)), 1.0, 0.0).astype(F32)


def ridge_inverse(gg):
    eye = twin_eye()
    left = lanes((64, 128)) < 64
    rows = sublanes((64, 128))
    m = jnp.where(left, gg + RIDGE * eye, eye)
    for k in range(RANK):
        col = jnp.broadcast_to(m[:, k : k + 1], (64, 128))
        prow = m[k : k + 1, :] / col[k : k + 1, :]
        m = jnp.where(rows == k, prow, m - col * prow)
    return jnp.where(left, roll64(m), m)


def split(x):
    hi = x.astype(BF16)
    return hi, (x - hi.astype(F32)).astype(BF16)


def split3(x):
    hi, lo = split(x)
    rest = x - hi.astype(F32) - lo.astype(F32)
    return hi, lo, rest.astype(BF16)


def factor_kernel(
    obs_hbm, u0_ref, v0_ref,
    ust, vst, u_out, v_out,
    obs, rh, rl, part, r1, r2, pan, gw, gi, qt2, gu, wl, wr, qs, rq, rg, qp, vn,
    gv1, gv2, gva, gvb, gua,
    obs_sem, s1s, s1r, s2s, s2r, ays, ayr, acs, acr,
    g1s, g1r, g2s, g2r, qs_s, qs_r, rg_s, rg_r, qa_s, qa_r, v0s, v0r,
):
    row = lax.axis_index("rows")
    col = lax.axis_index("cols")
    y, zh, co = col // 4, (col // 2) % 2, col % 2

    def cid(yy, zz, cc):
        return yy * 4 + zz * 2 + cc

    def pos(cc, yy, zz):
        return cc * 8 + yy * 2 + zz

    def to_chip(k):
        return (y + 1 + k // 2) % NY, (zh + 1 + k) % 2

    def from_chip(k):
        return (y + 2 * NY - 1 - k // 2) % NY, (zh + 1 + k) % 2

    sib = {"cols": cid(y, zh, 1 - co)}

    def chip(k):
        yy, zz = to_chip(k)
        return {"cols": cid(yy, zz, co)}

    def rpeer(d):
        return {"rows": lax.rem(row + d, NR)}

    def rcopy(src, dst, ssem, rsem, dev):
        return pltpu.make_async_remote_copy(
            src_ref=src, dst_ref=dst, send_sem=ssem, recv_sem=rsem, device_id=dev, device_id_type=MESH
        )

    load = pltpu.make_async_copy(obs_hbm, obs, obs_sem)
    load.start()

    barrier = pltpu.get_barrier_semaphore()
    peers = [sib] + [chip(k) for k in range(7)] + [rpeer(d) for d in range(1, NR)]
    for dev in peers:
        pl.semaphore_signal(barrier, inc=1, device_id=dev, device_id_type=MESH)
    pl.semaphore_wait(barrier, len(peers))

    own = pos(co, y, zh)
    left256 = (lanes((HALF, 256)) % 128) < 64

    def set_apply(inv2):
        zero = jnp.zeros_like(inv2)
        g = jnp.concatenate(
            [jnp.concatenate([inv2, zero], axis=1), jnp.concatenate([zero, inv2], axis=1)], axis=0
        )
        g1, g2, g3 = split3(g)
        gw[0] = jnp.concatenate([g1, g1], axis=0)
        gw[1] = jnp.concatenate([g2, g2], axis=0)
        gw[2] = jnp.concatenate([g3, g1], axis=0)

    def solved(slot):
        p1, p2, p3 = split3(pan[slot])
        p12 = jnp.concatenate([p1, p2], axis=1)
        p13 = jnp.concatenate([p1, p3], axis=1)
        return dot(p12, gw[0]) + (dot(p12, gw[1]) + dot(p13, gw[2]))

    def apply_chunk(slot, j, buf):
        hi, lo = split(solved(slot))
        st = jnp.where(left256, hi.astype(F32), lo.astype(F32))
        us = jnp.concatenate([st[:, :128], st[:, 128:]], axis=0)
        ust[buf, pl.ds(pl.multiple_of(j * CH, CH), CH), :] = us.astype(BF16)
        return us

    def apply_chunks(chunks, buf):
        for slot, j in chunks:
            apply_chunk(slot, j, buf)

    def time_chunks(chunks, buf):
        left, right, grams = [], [], []
        for slot, j in chunks:
            rows = pl.ds(pl.multiple_of(j * CH, CH), CH)
            us = apply_chunk(slot, j, buf)
            ut = us.T.astype(BF16)
            left += [ut, ut]
            right += [rh[rows, :], rl[rows, :]]
            grams.append(dot(ut, us.astype(BF16)))
        gu[...] += sum(grams)
        qt2[...] += dot(jnp.concatenate(left, axis=1), jnp.concatenate(right, axis=0))

    def gather_cols(process, buf):
        def chunk(k, cc):
            yy, zz = from_chip(k)
            return pos(cc, yy, zz), cid(yy, zz, cc)

        for k in range(7):
            rcopy(pan.at[own], pan.at[own], ays.at[k], ayr.at[k], chip(k)).start()
        rcopy(pan.at[own], pan.at[own], acs.at[7], acr.at[7], sib).start()
        process([(own, cid(y, zh, co))], buf)

        def arrive(k, carry):
            p, j = chunk(k, co)
            rcopy(pan.at[p], pan.at[p], ays.at[k], ayr.at[k], sib).wait_recv()
            rcopy(pan.at[p], pan.at[p], acs.at[k], acr.at[k], sib).start()
            b = (k + 7) % 8
            ps, js = chunk(b, 1 - co)
            rcopy(pan.at[ps], pan.at[ps], acs.at[b], acr.at[b], sib).wait_recv()
            process([(p, j), (ps, js)], buf)
            return carry

        lax.fori_loop(0, 7, arrive, 0)
        ps, js = chunk(6, 1 - co)
        rcopy(pan.at[ps], pan.at[ps], acs.at[6], acr.at[6], sib).wait_recv()
        process([(ps, js)], buf)

        def drain(k, carry):
            rcopy(pan.at[own], pan.at[own], ays.at[k], ayr.at[k], sib).wait_send()
            rcopy(pan.at[own], pan.at[own], acs.at[k], acr.at[k], sib).wait_send()
            return carry

        lax.fori_loop(0, 7, drain, 0)
        rcopy(pan.at[own], pan.at[own], acs.at[7], acr.at[7], sib).wait_send()

    def time_factor():
        return dot(gi[:, :RANK], qp[...].reshape(RANK, NT_LOC), precision=HI)

    def series_chunks(chunks, buf):
        for slot, j in chunks:
            rows = pl.ds(pl.multiple_of(j * CH, CH), CH)
            us = ust[buf, rows, :]
            low = dot(jnp.concatenate([us, us], axis=1), vst[buf, :, :])
            remain = low + jnp.clip(obs[rows, :] - low, -SHRINK, SHRINK)
            hi, lo = split(remain)
            rh[rows, :] = hi
            rl[rows, :] = lo
            a = dot(jnp.concatenate([hi[:HALF], lo[:HALF]], axis=0), wl[...])
            b = dot(jnp.concatenate([hi[HALF:], lo[HALF:]], axis=0), wr[...])
            s = a + b
            s = s[:, :128] + s[:, 128:]
            part[slot] = s[:HALF] + s[HALF:]

    vn[row] = jnp.zeros((64, 128), F32)
    vn[row, :, pl.ds(0, RANK)] = v0_ref[...]
    for d in range(1, NR):
        rcopy(vn.at[row], vn.at[row], v0s.at[d - 1], v0r.at[d - 1], rpeer(d)).start()
    pan[own] = jnp.concatenate([u0_ref[:, :HALF], u0_ref[:, HALF:]], axis=0).T
    set_apply(twin_eye())
    gather_cols(apply_chunks, 0)
    for d in range(1, NR):
        src = lax.rem(row + NR - d, NR)
        rcopy(vn.at[row], vn.at[src], v0s.at[d - 1], v0r.at[d - 1], rpeer(d)).wait()
    qp[...] = vn[...].reshape(NT_LOC, 128).T[:RANK].reshape(NR, 8, NT_LOC)
    gi[...] = twin_eye()
    load.wait()

    def iteration(t, carry):
        buf = lax.rem(t, 2)
        nxt = 1 - buf
        vh, vl = split(time_factor())
        pair = jnp.concatenate([vh, vl], axis=0)
        gva[...] = pack_gram(dot(pair, pair, dims=((1,), (1,))))
        rcopy(gva, gv1, g1s, g1r, sib).start()
        vst[buf, :, :] = jnp.concatenate([vh, vh, vl, vl], axis=0)
        x = pair.astype(F32).T
        xr = roll64(x)
        left = lanes((NT_LOC, 128)) < 64
        zero = jnp.zeros_like(x)
        wl[...] = jnp.concatenate([jnp.where(left, x, zero), jnp.where(left, xr, zero)], axis=1).astype(BF16)
        wr[...] = jnp.concatenate([jnp.where(left, zero, xr), jnp.where(left, zero, x)], axis=1).astype(BF16)

        def two(i, cc):
            out = []
            for e in range(2):
                yy, zz = to_chip(2 * i + e)
                out.append((pos(cc, yy, zz), cid(yy, zz, cc)))
            return out

        def to_sib(i, c):
            chunks = two(i, 1 - co)
            series_chunks(chunks, buf)
            for e in range(2):
                k = 2 * i + e
                rcopy(part.at[chunks[e][0]], r1.at[k], s1s.at[k], s1r.at[k], sib).start()

            @pl.when(i == 1)
            def _():
                rcopy(gva, gv1, g1s, g1r, sib).wait()
                gvb[...] = gva[...] + gv1[...]
                for k in range(7):
                    rcopy(gvb, gv2.at[k], g2s.at[k], g2r.at[k], chip(k)).start()

            return c

        lax.fori_loop(0, NY, to_sib, 0)

        def own_core(i):
            chunks = two(i, co)
            series_chunks(chunks, buf)
            for e in range(2):
                k = 2 * i + e
                slot = chunks[e][0]
                rcopy(part.at[slot], r1.at[k], s1s.at[k], s1r.at[k], sib).wait_recv()
                part[slot] += r1[k]
            return chunks

        def to_owner(i, c):
            chunks = own_core(i)
            for e in range(2):
                k = 2 * i + e
                rcopy(part.at[chunks[e][0]], r2.at[k], s2s.at[k], s2r.at[k], chip(k)).start()
            return c

        lax.fori_loop(0, NY - 1, to_owner, 0)
        chunks = own_core(NY - 1)
        rcopy(part.at[chunks[0][0]], r2.at[6], s2s.at[6], s2r.at[6], chip(6)).start()

        gu[...] = jnp.zeros_like(gu)
        qt2[...] = jnp.zeros_like(qt2)
        g = gvb[...]
        for k in range(7):
            rcopy(gvb, gv2.at[k], g2s.at[k], g2r.at[k], chip(k)).wait()
            g += gv2[k]
        set_apply(ridge_inverse(unpack_gram(g)))

        s = part[own]
        for k in range(7):
            rcopy(part.at[own], r2.at[k], s2s.at[k], s2r.at[k], chip(k)).wait_recv()
            s += r2[k]
        pan[own] = s

        gather_cols(time_chunks, nxt)

        def drain(k, c):
            rcopy(part.at[own], r1.at[k], s1s.at[k], s1r.at[k], sib).wait_send()
            return c

        lax.fori_loop(0, 8, drain, 0)
        for k in range(7):
            rcopy(part.at[own], r2.at[k], s2s.at[k], s2r.at[k], sib).wait_send()

        gua[...] = pack_gram(gu[...])
        for d in range(1, NR):
            rcopy(gua, rg.at[d - 1], rg_s.at[d - 1], rg_r.at[d - 1], rpeer(d)).start()
        q = qt2[...]
        qs[...] = (q[:64] + q[64:]).reshape(NR, 8, NT_LOC)
        for d in range(1, NR):
            peer = lax.rem(row + d, NR)
            rcopy(qs.at[peer], rq.at[d - 1], qs_s.at[d - 1], qs_r.at[d - 1], rpeer(d)).start()
        acc = qs[row]
        g = gua[...]
        for d in range(1, NR):
            rcopy(gua, rg.at[d - 1], rg_s.at[d - 1], rg_r.at[d - 1], rpeer(d)).wait()
            g += rg[d - 1]
        for d in range(1, NR):
            peer = lax.rem(row + d, NR)
            rcopy(qs.at[peer], rq.at[d - 1], qs_s.at[d - 1], qs_r.at[d - 1], rpeer(d)).wait()
            acc += rq[d - 1]
        qp[row] = acc
        for d in range(1, NR):
            rcopy(qp.at[row], qp.at[row], qa_s.at[d - 1], qa_r.at[d - 1], rpeer(d)).start()
        gi[...] = ridge_inverse(unpack_gram(g))
        for d in range(1, NR):
            src = lax.rem(row + NR - d, NR)
            rcopy(qp.at[row], qp.at[src], qa_s.at[d - 1], qa_r.at[d - 1], rpeer(d)).wait()
        return carry

    lax.fori_loop(0, ITERS, iteration, 0)

    u2 = solved(own)
    u_out[:, pl.ds(0, HALF)] = u2[:, :128].T[:RANK]
    u_out[:, pl.ds(HALF, HALF)] = u2[:, 128:].T[:RANK]
    vt = time_factor()
    vh, vl = split(vt)
    vst[ITERS % 2, :, :] = jnp.concatenate([vh, vh, vl, vl], axis=0)
    vn[...] = jnp.concatenate([vt, vt], axis=0).T.reshape(NR, 64, 128)
    v_out[...] = vn[row, :, pl.ds(0, RANK)]


def factors(observed, ut, v):
    vm = pl.BlockSpec(memory_space=pltpu.VMEM)
    dma = pltpu.SemaphoreType.DMA
    return pl.pallas_call(
        factor_kernel,
        out_shape=(
            jax.ShapeDtypeStruct((2, NS_LOC, 128), BF16),
            jax.ShapeDtypeStruct((2, 256, NT_LOC), BF16),
            jax.ShapeDtypeStruct((RANK, CH), F32),
            jax.ShapeDtypeStruct((64, RANK), F32),
        ),
        in_specs=[pl.BlockSpec(memory_space=pltpu.HBM), vm, vm],
        out_specs=(vm, vm, vm, vm),
        scratch_shapes=[
            pltpu.VMEM((NS_LOC, NT_LOC), F32),
            pltpu.VMEM((NS_LOC, NT_LOC), BF16),
            pltpu.VMEM((NS_LOC, NT_LOC), BF16),
            pltpu.VMEM((16, HALF, 128), F32),
            pltpu.VMEM((8, HALF, 128), F32),
            pltpu.VMEM((7, HALF, 128), F32),
            pltpu.VMEM((16, HALF, 128), F32),
            pltpu.VMEM((3, 256, 256), BF16),
            pltpu.VMEM((64, 128), F32),
            pltpu.VMEM((128, NT_LOC), F32),
            pltpu.VMEM((128, 128), F32),
            pltpu.VMEM((NT_LOC, 256), BF16),
            pltpu.VMEM((NT_LOC, 256), BF16),
            pltpu.VMEM((NR, 8, NT_LOC), F32),
            pltpu.VMEM((NR - 1, 8, NT_LOC), F32),
            pltpu.VMEM((NR - 1, 32, 128), F32),
            pltpu.VMEM((NR, 8, NT_LOC), F32),
            pltpu.VMEM((NR, 64, 128), F32),
            pltpu.VMEM((32, 128), F32),
            pltpu.VMEM((7, 32, 128), F32),
            pltpu.VMEM((32, 128), F32),
            pltpu.VMEM((32, 128), F32),
            pltpu.VMEM((32, 128), F32),
            dma,
            dma((8,)), dma((8,)), dma((7,)), dma((7,)), dma((7,)), dma((7,)), dma((8,)), dma((8,)),
            dma, dma, dma((7,)), dma((7,)),
            dma((7,)), dma((7,)), dma((7,)), dma((7,)), dma((7,)), dma((7,)), dma((7,)), dma((7,)),
        ],
        compiler_params=pltpu.CompilerParams(
            collective_id=0, has_side_effects=True, vmem_limit_bytes=FACTOR_VMEM * 1024 * 1024
        ),
        name="factor_updates",
    )(observed, ut, v)


def slabs_kernel(obs_ref, us_ref, vs_ref, u_ref, v_ref, low_ref, sparse_ref, u_out, v_out):
    def low(k):
        us = us_ref[k]
        return dot(jnp.concatenate([us, us], axis=1), vs_ref[k])

    low_ref[...] = low(0)
    diff = obs_ref[...] - low(1)
    sparse_ref[...] = diff - jnp.clip(diff, -SHRINK, SHRINK)
    u_out[...] = u_ref[...]
    v_out[...] = v_ref[...]


def slabs(observed, ust, vst, u, v):
    block = 512
    wide = pl.BlockSpec((block, NT_LOC), lambda i: (i, 0))
    u_spec = pl.BlockSpec((RANK, CH), lambda i: (0, 0))
    v_spec = pl.BlockSpec((64, RANK), lambda i: (0, 0))
    slab = jax.ShapeDtypeStruct((NS_LOC, NT_LOC), F32)
    return pl.pallas_call(
        slabs_kernel,
        grid=(NS_LOC // block,),
        out_shape=(slab, slab, jax.ShapeDtypeStruct((RANK, CH), F32), jax.ShapeDtypeStruct((64, RANK), F32)),
        in_specs=[
            wide,
            pl.BlockSpec((2, block, 128), lambda i: (0, i, 0)),
            pl.BlockSpec((2, 256, NT_LOC), lambda i: (0, 0, 0)),
            u_spec,
            v_spec,
        ],
        out_specs=(wide, wide, u_spec, v_spec),
        compiler_params=pltpu.CompilerParams(vmem_limit_bytes=SLABS_VMEM * 1024 * 1024),
        name="final_slabs",
    )(observed, ust, vst, u, v)


def shards(observed, u_start, v_start):
    ust, vst, ut, v_own = factors(observed, u_start.T, v_start)
    low, sparse, ut, v_own = slabs(observed, ust, vst, ut, v_own)
    return (low, sparse, ut.T, v_own)


def solution(mesh):
    return jax.shard_map(
        shards,
        mesh=mesh,
        in_specs=(P("rows", "cols"), P(("rows", "cols"), None), P(("cols", "rows"), None)),
        out_specs=(
            P("rows", "cols"),
            P("rows", "cols"),
            P(("rows", "cols"), None),
            P(("cols", "rows"), None),
        ),
        check_vma=False,
    )
```

time: 236 us -> 206 us (0.87)
  Pallas kernels: 226 us -> 200 us
    pallas_call x1, Pallas kernels: 219 us -> 192 us  [factors(): pl.pallas_call(factor_kernel, out_shape=(jax.ShapeDtypeStruct((2, NS_LOC,...]
where the time goes in v2:
time: 206 us; the launch traced here: 205 us
  Pallas kernels  200 us (97%)
  local copies, waits for them, and re-layouts  4.97 us (2%)
    pallas_call x1, Pallas kernels, factors(): pl.pallas_call(factor_kernel, out_shape=(jax.ShapeDtypeStruct((2, NS_LOC,...  192 us
    pallas_call x1, Pallas kernels, slabs(): pl.pallas_call(slabs_kernel, grid=(NS_LOC // block,), out_shape=(slab, sl...  7.24 us
    unnamed x8, local copies, waits for them, and re-layouts  4.97 us

profile of v2, /device:TPU:0, one launch (start us, length us, event | category | flops | bytes accessed | tf_op | source)
XLA Modules:
  0.0 205.3 jit_solution(14926653526557027504)
XLA Ops:
  0.6 0.0 copy-start
  0.6 3.4 %copy-done = f32[4096,512]{1,0:T(8,128)S(1)} copy-done((f32[4096,512]{1,0:T(8,128)S(1)}, f32[4096,512]{1,0:T(8,128)}, u32[]{:S(2)}) %copy-start) | copy-done | bytes 8388632
  4.0 0.0 copy-start.2
  4.0 0.8 copy-done.2
  4.9 0.0 copy-start.3
  4.9 0.8 copy-done.3
  5.6 0.0 copy-start.1
  5.6 192.4 %factor_updates.1 = (bf16[2,4096,128]{2,1,0:T(8,128)(2,1)S(1)}, bf16[2,256,512]{2,1,0:T(8,128)(2,1)S(1)}, f32[64,256]{1,0:T(8,128)S(1)}, f32[64,64]{1,0:T(8,128)S(1)}) custom-call(f32[4096,512]{1,0:T(8,128)S(1)} %copy-done, f32[64,256]{1,0:T(8,128)S(1)} %bitcast.2, f32[64,64]{1,0:T(8,128)S(1)} %copy-done.3), custom_call_target="tpu_custom_call" | custom-call | tf_op jit(solution)/shard_map/factor_updates/pallas_call | solution.py:363
  198.0 0.0 copy-done.1
  198.0 7.2 %final_slabs.1 = (f32[4096,512]{1,0:T(8,128)}, f32[4096,512]{1,0:T(8,128)}, f32[64,256]{1,0:T(8,128)}, f32[64,64]{1,0:T(8,128)}) custom-call(f32[4096,512]{1,0:T(8,128)S(1)} %copy-done.1, bf16[2,4096,128]{2,1,0:T(8,128)(2,1)S(1)} %get-tuple-element.12.us_ref, bf16[2,256,512]{2,1,0:T(8,128)(2,1)S(1)} %get-tuple-element.13.vs_ref, ...), custom_call_target="tpu_custom_call" | custom-call | tf_op jit(solution)/shard_map/final_slabs/pallas_call | solution.py:427
Async XLA Ops:
  0.6 3.4 %copy-start = (f32[4096,512]{1,0:T(8,128)S(1)}, f32[4096,512]{1,0:T(8,128)}, u32[]{:S(2)}) copy-start(f32[4096,512]{1,0:T(8,128)} %obs_ref.1) | copy-start | bytes 25165828
  4.0 0.8 copy-start.2
  4.9 0.8 copy-start.3
  5.6 192.4 %copy-start.1 = (f32[4096,512]{1,0:T(8,128)S(1)}, f32[4096,512]{1,0:T(8,128)}, u32[]{:S(2)}) copy-start(f32[4096,512]{1,0:T(8,128)} %obs_ref.1) | copy-start | bytes 25165828

commit v3 on v2

v3 whole, which is shorter than its diff:
```python
import functools

import jax
import jax.numpy as jnp
from jax import lax
from jax.experimental import pallas as pl
from jax.experimental.pallas import tpu as pltpu
from jax.sharding import PartitionSpec as P

ITERS = 4
SHRINK = 0.5
RIDGE = 1.0
RANK = 64
NY = 4
NR = 8
CH = 256
HALF = CH // 2
SUB = HALF // 2
NT_LOC = 512
NS_LOC = 4096
FACTOR_VMEM = 48
SLABS_VMEM = 16
MESH = pl.DeviceIdType.MESH
HI = lax.Precision.HIGHEST
F32 = jnp.float32
BF16 = jnp.bfloat16


def dot(a, b, dims=((1,), (0,)), precision=None):
    return lax.dot_general(a, b, (dims, ((), ())), precision=precision, preferred_element_type=F32)


def lanes(shape):
    return lax.broadcasted_iota(jnp.int32, shape, len(shape) - 1)


def sublanes(shape):
    return lax.broadcasted_iota(jnp.int32, shape, len(shape) - 2)


def roll64(m):
    return pltpu.roll(m, 64, 1)


def pack_gram(m):
    s = m + roll64(m)
    t = s[:64] + s[64:]
    return jnp.where(lanes((32, 128)) < 64, t[:32], t[32:])


def unpack_gram(k):
    kr = roll64(k)
    left = lanes((32, 128)) < 64
    return jnp.concatenate([jnp.where(left, k, kr), jnp.where(left, kr, k)], axis=0)


def twin_eye():
    return jnp.where((lanes((64, 128)) % 64) == sublanes((64, 128)), 1.0, 0.0).astype(F32)


def ridge_inverse(gg):
    eye = twin_eye()
    left = lanes((64, 128)) < 64
    rows = sublanes((64, 128))
    m = jnp.where(left, gg + RIDGE * eye, eye)
    for k in range(0, RANK, 2):
        c0 = jnp.broadcast_to(m[:, k : k + 1], (64, 128))
        c1 = jnp.broadcast_to(m[:, k + 1 : k + 2], (64, 128))
        r0, r1 = m[k : k + 1, :], m[k + 1 : k + 2, :]
        a, b = c0[k : k + 1, :], c1[k : k + 1, :]
        d, e = c0[k + 1 : k + 2, :], c1[k + 1 : k + 2, :]
        scale = 1.0 / (a * e - b * d)
        n0 = (e * r0 - b * r1) * scale
        n1 = (a * r1 - d * r0) * scale
        m = jnp.where(rows == k, n0, jnp.where(rows == k + 1, n1, m - c0 * n0 - c1 * n1))
    return jnp.where(left, roll64(m), m)


def split(x):
    hi = x.astype(BF16)
    return hi, (x - hi.astype(F32)).astype(BF16)


def split3(x):
    hi, lo = split(x)
    rest = x - hi.astype(F32) - lo.astype(F32)
    return hi, lo, rest.astype(BF16)


def factor_kernel(
    obs_hbm, u0_hbm, v0_hbm,
    ust, vst, u_out, v_out,
    obs, rh, rl, part, r1, r2, pan, gw, gi, qt2, gu, wl, wr, qs, rq, rg, qp, vn,
    gv1, gv2, gva, gvb, gua, u0_ref, v0_ref,
    obs_sem, u0_sem, v0_sem, s1s, s1r, s2s, s2r, ays, ayr, acs, acr,
    g1s, g1r, g2s, g2r, qs_s, qs_r, rg_s, rg_r, qa_s, qa_r, v0s, v0r,
):
    row = lax.axis_index("rows")
    col = lax.axis_index("cols")
    y, zh, co = col // 4, (col // 2) % 2, col % 2

    def cid(yy, zz, cc):
        return yy * 4 + zz * 2 + cc

    def pos(cc, yy, zz):
        return cc * 8 + yy * 2 + zz

    def to_chip(k):
        return (y + 1 + k // 2) % NY, (zh + 1 + k) % 2

    sib = {"cols": cid(y, zh, 1 - co)}

    def chip(k):
        yy, zz = to_chip(k)
        return {"cols": cid(yy, zz, co)}

    def rpeer(d):
        return {"rows": lax.rem(row + d, NR)}

    def rcopy(src, dst, ssem, rsem, dev):
        return pltpu.make_async_remote_copy(
            src_ref=src, dst_ref=dst, send_sem=ssem, recv_sem=rsem, device_id=dev, device_id_type=MESH
        )

    load_u = pltpu.make_async_copy(u0_hbm, u0_ref, u0_sem)
    load_u.start()
    load_v = pltpu.make_async_copy(v0_hbm, v0_ref, v0_sem)
    load_v.start()
    load = pltpu.make_async_copy(obs_hbm, obs, obs_sem)
    load.start()

    barrier = pltpu.get_barrier_semaphore()
    peers = [sib] + [chip(k) for k in range(7)] + [rpeer(d) for d in range(1, NR)]
    for dev in peers:
        pl.semaphore_signal(barrier, inc=1, device_id=dev, device_id_type=MESH)
    pl.semaphore_wait(barrier, len(peers))

    own = pos(co, y, zh)

    def slab_list(cc, h):
        first = [cid(n // 2, n % 2, cc) * CH + h * SUB for n in range(8)]
        return [pl.ds(pl.multiple_of(f + o, SUB), SUB) for o in (0, HALF) for f in first]

    def rows_of(ref, slabs, *lead):
        return jnp.concatenate([ref[(*lead, q, slice(None))] for q in slabs], axis=0)

    def put_rows(ref, slabs, value, *lead):
        for n, q in enumerate(slabs):
            ref[(*lead, q, slice(None))] = value[n * SUB : (n + 1) * SUB]

    def eight(cc):
        return pl.ds(pl.multiple_of(cc * 8, 8), 8)

    def set_apply(inv2):
        zero = jnp.zeros_like(inv2)
        g = jnp.concatenate(
            [jnp.concatenate([inv2, zero], axis=1), jnp.concatenate([zero, inv2], axis=1)], axis=0
        )
        g1, g2, g3 = split3(g)
        gw[0] = jnp.concatenate([g1, g1], axis=0)
        gw[1] = jnp.concatenate([g2, g2], axis=0)
        gw[2] = jnp.concatenate([g3, g1], axis=0)

    def solved(packed):
        p1, p2, p3 = split3(packed)
        p12 = jnp.concatenate([p1, p2], axis=1)
        p13 = jnp.concatenate([p1, p3], axis=1)
        return dot(p12, gw[0]) + (dot(p12, gw[1]) + dot(p13, gw[2]))

    def apply_chunks(cc, h, buf):
        u2 = solved(pan[h, eight(cc)].reshape(8 * SUB, 128))
        hi, lo = split(u2)
        left = (lanes(u2.shape) % 128) < 64
        st = jnp.where(left, hi.astype(F32), lo.astype(F32))
        us = jnp.concatenate([st[:, :128], st[:, 128:]], axis=0)
        slabs = slab_list(cc, h)
        put_rows(ust, slabs, us.astype(BF16), buf)
        return us, slabs

    def time_chunks(cc, h, buf):
        us, slabs = apply_chunks(cc, h, buf)
        ut = us.T.astype(BF16)
        gu[...] += dot(ut, us.astype(BF16))
        right = jnp.concatenate([rows_of(rh, slabs), rows_of(rl, slabs)], axis=0)
        qt2[...] += dot(jnp.concatenate([ut, ut], axis=1), right)

    def wait_recv(dst, rsem):
        rcopy(dst, dst, rsem, rsem, sib).wait_recv()

    def wait_send(src, ssem):
        rcopy(src, src, ssem, ssem, sib).wait_send()

    def gather_start(h):
        mine = pan.at[h, own]
        for k in range(7):
            rcopy(mine, mine, ays.at[h], ayr.at[h, k], chip(k)).start()

    def gather_finish(process, buf):
        def pair(g, cc):
            return pos(cc, (y + NY - g) % NY, 0)

        def half(h, carry):
            wait_recv(pan.at[h, pos(co, y, 1 - zh)], ayr.at[h, 6])
            block = pan.at[h, pl.ds(pair(0, co), 2)]
            rcopy(block, block, acs.at[h], acr.at[h, 0], sib).start()
            for g in range(1, NY):
                for e in range(2):
                    wait_recv(pan.at[h, pair(g, co) + e], ayr.at[h, 2 * (g - 1) + (zh + 1 + e) % 2])
                block = pan.at[h, pl.ds(pair(g, co), 2)]
                rcopy(block, block, acs.at[h], acr.at[h, g], sib).start()
            process(co, h, buf)
            for g in range(NY):
                wait_recv(pan.at[h, pl.ds(pair(g, 1 - co), 2)], acr.at[h, g])
            process(1 - co, h, buf)
            return carry

        lax.fori_loop(0, 2, half, 0)

    def drain_cols():
        for h in range(2):
            wait_send(pan.at[h, pl.ds(0, 7)], ays.at[h])
            wait_send(pan.at[h, pl.ds(0, 8)], acs.at[h])

    def time_factor():
        return dot(gi[:, :RANK], qp[...].reshape(RANK, NT_LOC), precision=HI)

    def series_chunks(cc, h, buf):
        slabs = slab_list(cc, h)
        n = 8 * SUB
        us = rows_of(ust, slabs, buf)
        low = dot(jnp.concatenate([us, us], axis=1), vst[buf, :, :])
        remain = low + jnp.clip(rows_of(obs, slabs) - low, -SHRINK, SHRINK)
        hi, lo = split(remain)
        put_rows(rh, slabs, hi)
        put_rows(rl, slabs, lo)
        a = dot(jnp.concatenate([hi[:n], lo[:n]], axis=0), wl[...])
        b = dot(jnp.concatenate([hi[n:], lo[n:]], axis=0), wr[...])
        s = a + b
        s = s[:, :128] + s[:, 128:]
        part[h, eight(cc)] = (s[:n] + s[n:]).reshape(8, SUB, 128)

    load_v.wait()
    vn[row] = jnp.zeros((64, 128), F32)
    vn[row, :, pl.ds(0, RANK)] = v0_ref[...]
    for d in range(1, NR):
        rcopy(vn.at[row], vn.at[row], v0s, v0r, rpeer(d)).start()
    load_u.wait()
    u0 = jnp.concatenate([u0_ref[:, :HALF], u0_ref[:, HALF:]], axis=0).T
    for h in range(2):
        pan[h, own] = u0[h * SUB : (h + 1) * SUB]
        gather_start(h)
    set_apply(twin_eye())
    gather_finish(apply_chunks, 0)
    drain_cols()
    wait_recv(vn.at[pl.ds(0, NR - 1)], v0r)
    wait_send(vn.at[pl.ds(0, NR - 1)], v0s)
    qp[...] = vn[...].reshape(NT_LOC, 128).T[:RANK].reshape(NR, 8, NT_LOC)
    gi[...] = twin_eye()
    load.wait()

    def iteration(t, carry):
        buf = lax.rem(t, 2)
        nxt = 1 - buf
        vh, vl = split(time_factor())
        pair = jnp.concatenate([vh, vl], axis=0)
        gva[...] = pack_gram(dot(pair, pair, dims=((1,), (1,))))
        rcopy(gva, gv1, g1s, g1r, sib).start()
        vst[buf, :, :] = jnp.concatenate([vh, vh, vl, vl], axis=0)
        x = pair.astype(F32).T
        xr = roll64(x)
        left = lanes((NT_LOC, 128)) < 64
        zero = jnp.zeros_like(x)
        wl[...] = jnp.concatenate([jnp.where(left, x, zero), jnp.where(left, xr, zero)], axis=1).astype(BF16)
        wr[...] = jnp.concatenate([jnp.where(left, zero, xr), jnp.where(left, zero, x)], axis=1).astype(BF16)

        def sums(h, carry):
            series_chunks(1 - co, h, buf)
            rcopy(part.at[h, eight(1 - co)], r1.at[h], s1s.at[h], s1r.at[h], sib).start()

            @pl.when(h == 0)
            def _():
                rcopy(gva, gv1, g1s, g1r, sib).wait()
                gvb[...] = gva[...] + gv1[...]
                for k in range(7):
                    rcopy(gvb, gv2.at[k], g2s, g2r, chip(k)).start()

            series_chunks(co, h, buf)
            wait_recv(r1.at[h], s1r.at[h])
            part[h, eight(co)] += r1[h]
            for k in range(7):
                yy, zz = to_chip(k)
                rcopy(part.at[h, pos(co, yy, zz)], r2.at[h, k], s2s.at[h], s2r.at[h], chip(k)).start()
            return carry

        lax.fori_loop(0, 2, sums, 0)

        def total(h):
            wait_recv(r2.at[h], s2r.at[h])
            pan[h, own] = part[h, own] + jnp.sum(r2[h], axis=0)
            gather_start(h)

        total(0)
        gu[...] = jnp.zeros_like(gu)
        qt2[...] = jnp.zeros_like(qt2)
        wait_recv(gv2, g2r)
        set_apply(ridge_inverse(unpack_gram(gvb[...] + jnp.sum(gv2[...], axis=0))))
        total(1)
        gather_finish(time_chunks, nxt)

        gua[...] = pack_gram(gu[...])
        for d in range(1, NR):
            rcopy(gua, rg.at[d - 1], rg_s, rg_r, rpeer(d)).start()
        q = qt2[...]
        qs[...] = (q[:64] + q[64:]).reshape(NR, 8, NT_LOC)
        for d in range(1, NR):
            peer = lax.rem(row + d, NR)
            rcopy(qs.at[peer], rq.at[d - 1], qs_s, qs_r, rpeer(d)).start()
        drain_cols()
        wait_send(gv2, g2s)
        for h in range(2):
            wait_send(r1.at[h], s1s.at[h])
            wait_send(r2.at[h], s2s.at[h])
        wait_recv(rg, rg_r)
        g = gua[...] + jnp.sum(rg[...], axis=0)
        wait_recv(rq, qs_r)
        qp[row] = qs[row] + jnp.sum(rq[...], axis=0)
        for d in range(1, NR):
            rcopy(qp.at[row], qp.at[row], qa_s, qa_r, rpeer(d)).start()
        gi[...] = ridge_inverse(unpack_gram(g))
        wait_send(rg, rg_s)
        wait_send(rq, qs_s)
        wait_recv(qp.at[pl.ds(0, NR - 1)], qa_r)
        wait_send(qp.at[pl.ds(0, NR - 1)], qa_s)
        return carry

    lax.fori_loop(0, ITERS, iteration, 0)

    u2 = solved(jnp.concatenate([pan[0, own], pan[1, own]], axis=0))
    u_out[:, pl.ds(0, HALF)] = u2[:, :128].T[:RANK]
    u_out[:, pl.ds(HALF, HALF)] = u2[:, 128:].T[:RANK]
    vt = time_factor()
    vh, vl = split(vt)
    vst[ITERS % 2, :, :] = jnp.concatenate([vh, vh, vl, vl], axis=0)
    vn[...] = jnp.concatenate([vt, vt], axis=0).T.reshape(NR, 64, 128)
    v_out[...] = vn[row, :, pl.ds(0, RANK)]


def factors(observed, ut, v):
    vm = pl.BlockSpec(memory_space=pltpu.VMEM)
    dma = pltpu.SemaphoreType.DMA
    return pl.pallas_call(
        factor_kernel,
        out_shape=(
            jax.ShapeDtypeStruct((2, NS_LOC, 128), BF16),
            jax.ShapeDtypeStruct((2, 256, NT_LOC), BF16),
            jax.ShapeDtypeStruct((RANK, CH), F32),
            jax.ShapeDtypeStruct((64, RANK), F32),
        ),
        in_specs=[pl.BlockSpec(memory_space=pl.ANY)] * 3,
        out_specs=(vm, vm, vm, vm),
        scratch_shapes=[
            pltpu.VMEM((NS_LOC, NT_LOC), F32),
            pltpu.VMEM((NS_LOC, NT_LOC), BF16),
            pltpu.VMEM((NS_LOC, NT_LOC), BF16),
            pltpu.VMEM((2, 16, SUB, 128), F32),
            pltpu.VMEM((2, 8, SUB, 128), F32),
            pltpu.VMEM((2, 7, SUB, 128), F32),
            pltpu.VMEM((2, 16, SUB, 128), F32),
            pltpu.VMEM((3, 256, 256), BF16),
            pltpu.VMEM((64, 128), F32),
            pltpu.VMEM((128, NT_LOC), F32),
            pltpu.VMEM((128, 128), F32),
            pltpu.VMEM((NT_LOC, 256), BF16),
            pltpu.VMEM((NT_LOC, 256), BF16),
            pltpu.VMEM((NR, 8, NT_LOC), F32),
            pltpu.VMEM((NR - 1, 8, NT_LOC), F32),
            pltpu.VMEM((NR - 1, 32, 128), F32),
            pltpu.VMEM((NR, 8, NT_LOC), F32),
            pltpu.VMEM((NR, 64, 128), F32),
            pltpu.VMEM((32, 128), F32),
            pltpu.VMEM((7, 32, 128), F32),
            pltpu.VMEM((32, 128), F32),
            pltpu.VMEM((32, 128), F32),
            pltpu.VMEM((32, 128), F32),
            pltpu.VMEM((RANK, CH), F32),
            pltpu.VMEM((64, RANK), F32),
            dma, dma, dma,
            dma((2,)), dma((2,)), dma((2,)), dma((2,)), dma((2,)), dma((2, 7)), dma((2,)), dma((2, 4)),
            dma, dma, dma, dma,
            dma, dma, dma, dma, dma, dma, dma, dma,
        ],
        compiler_params=pltpu.CompilerParams(
            collective_id=0, has_side_effects=True, vmem_limit_bytes=FACTOR_VMEM * 1024 * 1024
        ),
        cost_estimate=pl.CostEstimate(flops=13_000_000_000, bytes_accessed=12_000_000, transcendentals=0),
        name="factor_updates",
    )(observed, ut, v)


def slabs_kernel(obs_ref, us_ref, vs_ref, u_ref, v_ref, low_ref, sparse_ref, u_out, v_out):
    def low(k):
        us = us_ref[k]
        return dot(jnp.concatenate([us, us], axis=1), vs_ref[k])

    low_ref[...] = low(0)
    diff = obs_ref[...] - low(1)
    sparse_ref[...] = diff - jnp.clip(diff, -SHRINK, SHRINK)
    u_out[...] = u_ref[...]
    v_out[...] = v_ref[...]


def slabs(observed, ust, vst, u, v):
    block = 512
    wide = pl.BlockSpec((block, NT_LOC), lambda i: (i, 0))
    u_spec = pl.BlockSpec((RANK, CH), lambda i: (0, 0))
    v_spec = pl.BlockSpec((64, RANK), lambda i: (0, 0))
    slab = jax.ShapeDtypeStruct((NS_LOC, NT_LOC), F32)
    return pl.pallas_call(
        slabs_kernel,
        grid=(NS_LOC // block,),
        out_shape=(slab, slab, jax.ShapeDtypeStruct((RANK, CH), F32), jax.ShapeDtypeStruct((64, RANK), F32)),
        in_specs=[
            wide,
            pl.BlockSpec((2, block, 128), lambda i: (0, i, 0)),
            pl.BlockSpec((2, 256, NT_LOC), lambda i: (0, 0, 0)),
            u_spec,
            v_spec,
        ],
        out_specs=(wide, wide, u_spec, v_spec),
        compiler_params=pltpu.CompilerParams(vmem_limit_bytes=SLABS_VMEM * 1024 * 1024),
        name="final_slabs",
    )(observed, ust, vst, u, v)


def shards(observed, u_start, v_start):
    ust, vst, ut, v_own = factors(observed, u_start.T, v_start)
    low, sparse, ut, v_own = slabs(observed, ust, vst, ut, v_own)
    return (low, sparse, ut.T, v_own)


def solution(mesh):
    return jax.shard_map(
        shards,
        mesh=mesh,
        in_specs=(P("rows", "cols"), P(("rows", "cols"), None), P(("cols", "rows"), None)),
        out_specs=(
            P("rows", "cols"),
            P("rows", "cols"),
            P(("rows", "cols"), None),
            P(("cols", "rows"), None),
        ),
        check_vma=False,
    )
```

time: 206 us -> 176 us (0.85)
  Pallas kernels: 200 us -> 174 us
  local copies, waits for them, and re-layouts: 4.97 us -> 1.59 us
    pallas_call x1, Pallas kernels: 192 us -> 167 us  [factors(): pl.pallas_call(factor_kernel, out_shape=(jax.ShapeDtypeStruct((2, NS_LOC,...]
    unnamed x8 -> x6, local copies, waits for them, and re-layouts: 4.97 us -> 1.59 us
where the time goes in v3:
time: 176 us
  Pallas kernels  174 us (99%)
    pallas_call x1, Pallas kernels, factors(): pl.pallas_call(factor_kernel, out_shape=(jax.ShapeDtypeStruct((2, NS_LOC,...  167 us
    pallas_call x1, Pallas kernels, slabs(): pl.pallas_call(slabs_kernel, grid=(NS_LOC // block,), out_shape=(slab, sl...  7.24 us

profile of v3, /device:TPU:0, one launch (start us, length us, event | category | flops | bytes accessed | tf_op | source)
XLA Modules:
  0.0 176.2 jit_solution(17601090158260997003)
XLA Ops:
  0.6 0.0 copy-start.1
  0.6 0.8 copy-done.1
  1.5 0.0 copy-start.2
  1.5 0.8 copy-done.2
  2.2 0.0 copy-start
  2.2 166.7 %factor_updates.1 = (bf16[2,4096,128]{2,1,0:T(8,128)(2,1)S(1)}, bf16[2,256,512]{2,1,0:T(8,128)(2,1)S(1)}, f32[64,256]{1,0:T(8,128)S(1)}, f32[64,64]{1,0:T(8,128)S(1)}) custom-call(f32[4096,512]{1,0:T(8,128)} %obs_ref.1, f32[64,256]{1,0:T(8,128)S(1)} %bitcast.2, f32[64,64]{1,0:T(8,128)S(1)} %copy-done.2), custom_call_target="tpu_custom_call" | custom-call | flops 12999999488 | bytes 12000000 | tf_op jit(solution)/shard_map/factor_updates/pallas_call | solution.py:351
  168.9 0.0 copy-done
  168.9 7.2 %final_slabs.1 = (f32[4096,512]{1,0:T(8,128)}, f32[4096,512]{1,0:T(8,128)}, f32[64,256]{1,0:T(8,128)}, f32[64,64]{1,0:T(8,128)}) custom-call(f32[4096,512]{1,0:T(8,128)S(1)} %copy-done, bf16[2,4096,128]{2,1,0:T(8,128)(2,1)S(1)} %get-tuple-element.12.us_ref, bf16[2,256,512]{2,1,0:T(8,128)(2,1)S(1)} %get-tuple-element.13.vs_ref, ...), custom_call_target="tpu_custom_call" | custom-call | tf_op jit(solution)/shard_map/final_slabs/pallas_call | solution.py:418
Async XLA Ops:
  0.6 0.8 copy-start.1
  1.5 0.8 copy-start.2
  2.2 166.7 %copy-start = (f32[4096,512]{1,0:T(8,128)S(1)}, f32[4096,512]{1,0:T(8,128)}, u32[]{:S(2)}) copy-start(f32[4096,512]{1,0:T(8,128)} %obs_ref.1) | copy-start | bytes 25165828

commit v4 on v3

--- a/solution.py
+++ b/solution.py
@@ -58,22 +58,43 @@
     return jnp.where((lanes((64, 128)) % 64) == sublanes((64, 128)), 1.0, 0.0).astype(F32)
 
 
+def ridge_start(gg):
+    eye = twin_eye()
+    return jnp.where(lanes((64, 128)) < 64, gg + RIDGE * eye, eye)
+
+
+def ridge_steps(m, first, last):
+    rows = sublanes((64, 128))
+    for k in range(first, last, 4):
+        c = [jnp.broadcast_to(m[:, k + j : k + j + 1], (64, 128)) for j in range(4)]
+        r = [m[k + i : k + i + 1, :] for i in range(4)]
+        a = [[c[j][k + i : k + i + 1, :] for j in range(4)] for i in range(4)]
+
+        def two(a00, a01, a10, a11):
+            scale = 1.0 / (a00 * a11 - a01 * a10)
+            return lambda x, y: ((a11 * x - a01 * y) * scale, (a00 * y - a10 * x) * scale)
+
+        top = two(a[0][0], a[0][1], a[1][0], a[1][1])
+        n0, n1 = top(r[0], r[1])
+        t = [top(a[0][j], a[1][j]) for j in (2, 3)]
+        low = [r[i] - a[i][0] * n0 - a[i][1] * n1 for i in (2, 3)]
+        b = [[a[i][j] - a[i][0] * t[j - 2][0] - a[i][1] * t[j - 2][1] for j in (2, 3)] for i in (2, 3)]
+        n2, n3 = two(b[0][0], b[0][1], b[1][0], b[1][1])(low[0], low[1])
+        n0 = n0 - t[0][0] * n2 - t[1][0] * n3
+        n1 = n1 - t[0][1] * n2 - t[1][1] * n3
+        new = m - (c[0] * n0 + c[1] * n1) - (c[2] * n2 + c[3] * n3)
+        for i, n in enumerate((n0, n1, n2, n3)):
+            new = jnp.where(rows == k + i, n, new)
+        m = new
+    return m
+
+
+def ridge_end(m):
+    return jnp.where(lanes((64, 128)) < 64, roll64(m), m)
+
+
 def ridge_inverse(gg):
-    eye = twin_eye()
-    left = lanes((64, 128)) < 64
-    rows = sublanes((64, 128))
-    m = jnp.where(left, gg + RIDGE * eye, eye)
-    for k in range(0, RANK, 2):
-        c0 = jnp.broadcast_to(m[:, k : k + 1], (64, 128))
-        c1 = jnp.broadcast_to(m[:, k + 1 : k + 2], (64, 128))
-        r0, r1 = m[k : k + 1, :], m[k + 1 : k + 2, :]
-        a, b = c0[k : k + 1, :], c1[k : k + 1, :]
-        d, e = c0[k + 1 : k + 2, :], c1[k + 1 : k + 2, :]
-        scale = 1.0 / (a * e - b * d)
-        n0 = (e * r0 - b * r1) * scale
-        n1 = (a * r1 - d * r0) * scale
-        m = jnp.where(rows == k, n0, jnp.where(rows == k + 1, n1, m - c0 * n0 - c1 * n1))
-    return jnp.where(left, roll64(m), m)
+    return ridge_end(ridge_steps(ridge_start(gg), 0, RANK))
 
 
 def split(x):
@@ -91,9 +112,9 @@
     obs_hbm, u0_hbm, v0_hbm,
     ust, vst, u_out, v_out,
     obs, rh, rl, part, r1, r2, pan, gw, gi, qt2, gu, wl, wr, qs, rq, rg, qp, vn,
-    gv1, gv2, gva, gvb, gua, u0_ref, v0_ref,
+    gv1, gv2, gva, gvb, gvc, gua, guc, u0_ref, v0_ref,
     obs_sem, u0_sem, v0_sem, s1s, s1r, s2s, s2r, ays, ayr, acs, acr,
-    g1s, g1r, g2s, g2r, qs_s, qs_r, rg_s, rg_r, qa_s, qa_r, v0s, v0r,
+    g1s, g1r, g2s, g2r, g3s, g3r, g4s, g4r, qs_s, qs_r, rg_s, rg_r, qa_s, qa_r, v0s, v0r,
 ):
     row = lax.axis_index("rows")
     col = lax.axis_index("cols")
@@ -147,6 +168,8 @@
     def put_rows(ref, slabs, value, *lead):
         for n, q in enumerate(slabs):
             ref[(*lead, q, slice(None))] = value[n * SUB : (n + 1) * SUB]
+
+    my_half = pl.ds(pl.multiple_of(co * 16, 16), 16)
 
     def eight(cc):
         return pl.ds(pl.multiple_of(cc * 8, 8), 8)
@@ -172,15 +195,15 @@
         hi, lo = split(u2)
         left = (lanes(u2.shape) % 128) < 64
         st = jnp.where(left, hi.astype(F32), lo.astype(F32))
-        us = jnp.concatenate([st[:, :128], st[:, 128:]], axis=0)
+        us = jnp.concatenate([st[:, :128], st[:, 128:]], axis=0).astype(BF16)
         slabs = slab_list(cc, h)
-        put_rows(ust, slabs, us.astype(BF16), buf)
+        put_rows(ust, slabs, us, buf)
         return us, slabs
 
     def time_chunks(cc, h, buf):
         us, slabs = apply_chunks(cc, h, buf)
-        ut = us.T.astype(BF16)
-        gu[...] += dot(ut, us.astype(BF16))
+        ut = us.T
+        gu[...] += dot(ut, us)
         right = jnp.concatenate([rows_of(rh, slabs), rows_of(rl, slabs)], axis=0)
         qt2[...] += dot(jnp.concatenate([ut, ut], axis=1), right)
 
@@ -282,7 +305,7 @@
                 rcopy(gva, gv1, g1s, g1r, sib).wait()
                 gvb[...] = gva[...] + gv1[...]
                 for k in range(7):
-                    rcopy(gvb, gv2.at[k], g2s, g2r, chip(k)).start()
+                    rcopy(gvb.at[my_half], gv2.at[k], g2s, g2r, chip(k)).start()
 
             series_chunks(co, h, buf)
             wait_recv(r1.at[h], s1r.at[h])
@@ -299,17 +322,21 @@
             pan[h, own] = part[h, own] + jnp.sum(r2[h], axis=0)
             gather_start(h)
 
-        total(0)
         gu[...] = jnp.zeros_like(gu)
         qt2[...] = jnp.zeros_like(qt2)
         wait_recv(gv2, g2r)
-        set_apply(ridge_inverse(unpack_gram(gvb[...] + jnp.sum(gv2[...], axis=0))))
+        gvc[my_half] = gvb[my_half] + jnp.sum(gv2[...], axis=0)
+        swap = rcopy(gvc.at[my_half], gvc.at[my_half], g3s, g3r, sib)
+        swap.start()
+        total(0)
+        swap.wait()
+        set_apply(ridge_inverse(unpack_gram(gvc[...])))
         total(1)
         gather_finish(time_chunks, nxt)
 
         gua[...] = pack_gram(gu[...])
         for d in range(1, NR):
-            rcopy(gua, rg.at[d - 1], rg_s, rg_r, rpeer(d)).start()
+            rcopy(gua.at[my_half], rg.at[d - 1], rg_s, rg_r, rpeer(d)).start()
         q = qt2[...]
         qs[...] = (q[:64] + q[64:]).reshape(NR, 8, NT_LOC)
         for d in range(1, NR):
@@ -321,12 +348,15 @@
             wait_send(r1.at[h], s1s.at[h])
             wait_send(r2.at[h], s2s.at[h])
         wait_recv(rg, rg_r)
-        g = gua[...] + jnp.sum(rg[...], axis=0)
+        guc[my_half] = gua[my_half] + jnp.sum(rg[...], axis=0)
+        swap = rcopy(guc.at[my_half], guc.at[my_half], g4s, g4r, sib)
+        swap.start()
         wait_recv(rq, qs_r)
         qp[row] = qs[row] + jnp.sum(rq[...], axis=0)
         for d in range(1, NR):
             rcopy(qp.at[row], qp.at[row], qa_s, qa_r, rpeer(d)).start()
-        gi[...] = ridge_inverse(unpack_gram(g))
+        swap.wait()
+        gi[...] = ridge_inverse(unpack_gram(guc[...]))
         wait_send(rg, rg_s)
         wait_send(rq, qs_s)
         wait_recv(qp.at[pl.ds(0, NR - 1)], qa_r)
@@ -374,11 +404,13 @@
             pltpu.VMEM((NT_LOC, 256), BF16),
             pltpu.VMEM((NR, 8, NT_LOC), F32),
             pltpu.VMEM((NR - 1, 8, NT_LOC), F32),
-            pltpu.VMEM((NR - 1, 32, 128), F32),
+            pltpu.VMEM((NR - 1, 16, 128), F32),
             pltpu.VMEM((NR, 8, NT_LOC), F32),
             pltpu.VMEM((NR, 64, 128), F32),
             pltpu.VMEM((32, 128), F32),
-            pltpu.VMEM((7, 32, 128), F32),
+            pltpu.VMEM((7, 16, 128), F32),
+            pltpu.VMEM((32, 128), F32),
+            pltpu.VMEM((32, 128), F32),
             pltpu.VMEM((32, 128), F32),
             pltpu.VMEM((32, 128), F32),
             pltpu.VMEM((32, 128), F32),
@@ -386,7 +418,7 @@
             pltpu.VMEM((64, RANK), F32),
             dma, dma, dma,
             dma((2,)), dma((2,)), dma((2,)), dma((2,)), dma((2,)), dma((2, 7)), dma((2,)), dma((2, 4)),
-            dma, dma, dma, dma,
+            dma, dma, dma, dma, dma, dma, dma, dma,
             dma, dma, dma, dma, dma, dma, dma, dma,
         ],
         compiler_params=pltpu.CompilerParams(

time: 176 us -> 161 us (0.915)
  Pallas kernels: 174 us -> 159 us
    pallas_call x1, Pallas kernels: 167 us -> 152 us  [factors(): pl.pallas_call(factor_kernel, out_shape=(jax.ShapeDtypeStruct((2, NS_LOC,...]
where the time goes in v4:
time: 161 us
  Pallas kernels  159 us (99%)
    pallas_call x1, Pallas kernels, factors(): pl.pallas_call(factor_kernel, out_shape=(jax.ShapeDtypeStruct((2, NS_LOC,...  152 us
    pallas_call x1, Pallas kernels, slabs(): pl.pallas_call(slabs_kernel, grid=(NS_LOC // block,), out_shape=(slab, sl...  7.24 us

profile of v4, /device:TPU:0, one launch (start us, length us, event | category | flops | bytes accessed | tf_op | source)
XLA Modules:
  0.0 161.1 jit_solution(2393716246993783083)
XLA Ops:
  0.6 0.0 copy-start.1
  0.6 0.8 copy-done.1
  1.5 0.0 copy-start.2
  1.5 0.8 copy-done.2
  2.2 0.0 copy-start
  2.2 151.6 %factor_updates.1 = (bf16[2,4096,128]{2,1,0:T(8,128)(2,1)S(1)}, bf16[2,256,512]{2,1,0:T(8,128)(2,1)S(1)}, f32[64,256]{1,0:T(8,128)S(1)}, f32[64,64]{1,0:T(8,128)S(1)}) custom-call(f32[4096,512]{1,0:T(8,128)} %obs_ref.1, f32[64,256]{1,0:T(8,128)S(1)} %bitcast.2, f32[64,64]{1,0:T(8,128)S(1)} %copy-done.2), custom_call_target="tpu_custom_call" | custom-call | flops 12999999488 | bytes 12000000 | tf_op jit(solution)/shard_map/factor_updates/pallas_call | solution.py:381
  153.8 0.0 copy-done
  153.8 7.2 %final_slabs.1 = (f32[4096,512]{1,0:T(8,128)}, f32[4096,512]{1,0:T(8,128)}, f32[64,256]{1,0:T(8,128)}, f32[64,64]{1,0:T(8,128)}) custom-call(f32[4096,512]{1,0:T(8,128)S(1)} %copy-done, bf16[2,4096,128]{2,1,0:T(8,128)(2,1)S(1)} %get-tuple-element.12.us_ref, bf16[2,256,512]{2,1,0:T(8,128)(2,1)S(1)} %get-tuple-element.13.vs_ref, ...), custom_call_target="tpu_custom_call" | custom-call | tf_op jit(solution)/shard_map/final_slabs/pallas_call | solution.py:450
Async XLA Ops:
  0.6 0.8 copy-start.1
  1.5 0.8 copy-start.2
  2.2 151.6 %copy-start = (f32[4096,512]{1,0:T(8,128)S(1)}, f32[4096,512]{1,0:T(8,128)}, u32[]{:S(2)}) copy-start(f32[4096,512]{1,0:T(8,128)} %obs_ref.1) | copy-start | bytes 25165828

commit v5 on v4

--- a/solution.py
+++ b/solution.py
@@ -296,12 +296,11 @@
         wl[...] = jnp.concatenate([jnp.where(left, x, zero), jnp.where(left, xr, zero)], axis=1).astype(BF16)
         wr[...] = jnp.concatenate([jnp.where(left, zero, xr), jnp.where(left, zero, x)], axis=1).astype(BF16)
 
-        def sums(h, carry):
+        for h in range(2):
             series_chunks(1 - co, h, buf)
             rcopy(part.at[h, eight(1 - co)], r1.at[h], s1s.at[h], s1r.at[h], sib).start()
 
-            @pl.when(h == 0)
-            def _():
+            if h == 0:
                 rcopy(gva, gv1, g1s, g1r, sib).wait()
                 gvb[...] = gva[...] + gv1[...]
                 for k in range(7):
@@ -313,9 +312,6 @@
             for k in range(7):
                 yy, zz = to_chip(k)
                 rcopy(part.at[h, pos(co, yy, zz)], r2.at[h, k], s2s.at[h], s2r.at[h], chip(k)).start()
-            return carry
-
-        lax.fori_loop(0, 2, sums, 0)
 
         def total(h):
             wait_recv(r2.at[h], s2r.at[h])

time: 161 us -> 161 us (level)
  no operation moved by 1% of the time
where the time goes in v5:
time: 161 us
  Pallas kernels  158 us (98%)
    pallas_call x1, Pallas kernels, factors(): pl.pallas_call(factor_kernel, out_shape=(jax.ShapeDtypeStruct((2, NS_LOC,...  151 us
    pallas_call x1, Pallas kernels, slabs(): pl.pallas_call(slabs_kernel, grid=(NS_LOC // block,), out_shape=(slab, sl...  7.24 us

profile of v5, /device:TPU:0, one launch (start us, length us, event | category | flops | bytes accessed | tf_op | source)
XLA Modules:
  0.0 160.5 jit_solution(16533939834839225756)
XLA Ops:
  0.6 0.0 copy-start.1
  0.6 0.8 copy-done.1
  1.5 0.0 copy-start.2
  1.5 0.8 copy-done.2
  2.2 0.0 copy-start
  2.2 151.1 %factor_updates.1 = (bf16[2,4096,128]{2,1,0:T(8,128)(2,1)S(1)}, bf16[2,256,512]{2,1,0:T(8,128)(2,1)S(1)}, f32[64,256]{1,0:T(8,128)S(1)}, f32[64,64]{1,0:T(8,128)S(1)}) custom-call(f32[4096,512]{1,0:T(8,128)} %obs_ref.1, f32[64,256]{1,0:T(8,128)S(1)} %bitcast.2, f32[64,64]{1,0:T(8,128)S(1)} %copy-done.2), custom_call_target="tpu_custom_call" | custom-call | flops 12999999488 | bytes 12000000 | tf_op jit(solution)/shard_map/factor_updates/pallas_call | solution.py:377
  153.3 0.0 copy-done
  153.3 7.2 %final_slabs.1 = (f32[4096,512]{1,0:T(8,128)}, f32[4096,512]{1,0:T(8,128)}, f32[64,256]{1,0:T(8,128)}, f32[64,64]{1,0:T(8,128)}) custom-call(f32[4096,512]{1,0:T(8,128)S(1)} %copy-done, bf16[2,4096,128]{2,1,0:T(8,128)(2,1)S(1)} %get-tuple-element.12.us_ref, bf16[2,256,512]{2,1,0:T(8,128)(2,1)S(1)} %get-tuple-element.13.vs_ref, ...), custom_call_target="tpu_custom_call" | custom-call | tf_op jit(solution)/shard_map/final_slabs/pallas_call | solution.py:446
Async XLA Ops:
  0.6 0.8 copy-start.1
  1.5 0.8 copy-start.2
  2.2 151.1 %copy-start = (f32[4096,512]{1,0:T(8,128)S(1)}, f32[4096,512]{1,0:T(8,128)}, u32[]{:S(2)}) copy-start(f32[4096,512]{1,0:T(8,128)} %obs_ref.1) | copy-start | bytes 25165828

commit v6 on v5

--- a/solution.py
+++ b/solution.py
@@ -237,7 +237,8 @@
             process(1 - co, h, buf)
             return carry
 
-        lax.fori_loop(0, 2, half, 0)
+        for h in range(2):
+            half(h, 0)
 
     def drain_cols():
         for h in range(2):

time: 161 us -> 157 us (0.975)
  Pallas kernels: 158 us -> 155 us
    pallas_call x1, Pallas kernels: 151 us -> 147 us  [factors(): pl.pallas_call(factor_kernel, out_shape=(jax.ShapeDtypeStruct((2, NS_LOC,...]
where the time goes in v6:
time: 157 us
  Pallas kernels  155 us (99%)
  local copies, waits for them, and re-layouts  1.59 us (1%)
    pallas_call x1, Pallas kernels, factors(): pl.pallas_call(factor_kernel, out_shape=(jax.ShapeDtypeStruct((2, NS_LOC,...  147 us
    pallas_call x1, Pallas kernels, slabs(): pl.pallas_call(slabs_kernel, grid=(NS_LOC // block,), out_shape=(slab, sl...  7.24 us

profile of v6, /device:TPU:0, one launch (start us, length us, event | category | flops | bytes accessed | tf_op | source)
XLA Modules:
  0.0 156.9 jit_solution(8948741374826709602)
XLA Ops:
  0.6 0.0 copy-start.1
  0.6 0.8 copy-done.1
  1.5 0.0 copy-start.2
  1.5 0.8 copy-done.2
  2.2 0.0 copy-start
  2.2 147.4 %factor_updates.1 = (bf16[2,4096,128]{2,1,0:T(8,128)(2,1)S(1)}, bf16[2,256,512]{2,1,0:T(8,128)(2,1)S(1)}, f32[64,256]{1,0:T(8,128)S(1)}, f32[64,64]{1,0:T(8,128)S(1)}) custom-call(f32[4096,512]{1,0:T(8,128)} %obs_ref.1, f32[64,256]{1,0:T(8,128)S(1)} %bitcast.2, f32[64,64]{1,0:T(8,128)S(1)} %copy-done.2), custom_call_target="tpu_custom_call" | custom-call | flops 12999999488 | bytes 12000000 | tf_op jit(solution)/shard_map/factor_updates/pallas_call | solution.py:378
  149.7 0.0 copy-done
  149.7 7.2 %final_slabs.1 = (f32[4096,512]{1,0:T(8,128)}, f32[4096,512]{1,0:T(8,128)}, f32[64,256]{1,0:T(8,128)}, f32[64,64]{1,0:T(8,128)}) custom-call(f32[4096,512]{1,0:T(8,128)S(1)} %copy-done, bf16[2,4096,128]{2,1,0:T(8,128)(2,1)S(1)} %get-tuple-element.12.us_ref, bf16[2,256,512]{2,1,0:T(8,128)(2,1)S(1)} %get-tuple-element.13.vs_ref, ...), custom_call_target="tpu_custom_call" | custom-call | tf_op jit(solution)/shard_map/final_slabs/pallas_call | solution.py:447
Async XLA Ops:
  0.6 0.8 copy-start.1
  1.5 0.8 copy-start.2
  2.2 147.4 %copy-start = (f32[4096,512]{1,0:T(8,128)S(1)}, f32[4096,512]{1,0:T(8,128)}, u32[]{:S(2)}) copy-start(f32[4096,512]{1,0:T(8,128)} %obs_ref.1) | copy-start | bytes 25165828
